TPU v7x, 32 devices: a whole 2x2x4 slice. The times are simulated.
32 devices in a mesh: dp: 8 (over z, y), tensor: 4 (over x, core).
Axes of the slice: x: 2, y: 2, z: 4, core: 2. Of those that a mesh axis runs over, the one named last changes fastest.
Arguments:
- tokens: float32 [8192, 768], P(('dp', 'tensor')), may hold values from -6 to 6
- segments: int32 [8192], P('dp'), may hold values from 0 to 4, as said below
- routes: int32 [8192, 1], P('dp'), may hold values from 0 to 3
- cotangent: float32 [8192, 768], P(('dp', 'tensor')), may hold values from -6 to 6
- gain_attn: bfloat16 [768], replicated, may hold values from 0.5 to 1.5
- w_query: bfloat16 [768, 768], P('dp', 'tensor'), may hold values from -0.21875 to 0.21875
- w_key: bfloat16 [768, 768], P('dp', 'tensor'), may hold values from -0.21875 to 0.21875
- w_value: bfloat16 [768, 768], P('dp', 'tensor'), may hold values from -0.21875 to 0.21875
- w_output: bfloat16 [768, 768], P('tensor', 'dp'), may hold values from -0.875 to 0.875
- rel_table: bfloat16 [32, 12], replicated, may hold values from -4 to 4
- gain_ffn: bfloat16 [768], replicated, may hold values from 0.5 to 1.5
- w_router: bfloat16 [768, 4], replicated, may hold values from -0.15625 to 0.15625
- w_inner: bfloat16 [4, 768, 3072], P(None, 'dp', 'tensor'), may hold values from -0.21875 to 0.21875
- w_outer: bfloat16 [4, 3072, 768], P(None, 'tensor', 'dp'), may hold values from -0.3125 to 0.3125
Outputs:
- output: float32 [8192, 768], P(('dp', 'tensor'))
- grad_tokens: float32 [8192, 768], P(('dp', 'tensor'))
- grad_gain_attn: float32 [768], replicated
- grad_query: float32 [768, 768], P('dp', 'tensor')
- grad_key: float32 [768, 768], P('dp', 'tensor')
- grad_value: float32 [768, 768], P('dp', 'tensor')
- grad_output_proj: float32 [768, 768], P('tensor', 'dp')
- grad_table: float32 [32, 12], replicated
- grad_gain_ffn: float32 [768], replicated
- grad_router: float32 [768, 4], replicated
- grad_inner: float32 [4, 768, 3072], P(None, 'dp', 'tensor')
- grad_outer: float32 [4, 3072, 768], P(None, 'tensor', 'dp')
Inputs may be any that keep to these rules, and one draw needn't show every extreme that they name: `segments`: segment numbers start at 0 in each sequence of 1024 tokens and never fall within it; each sequence holds five documents.
All inputs are finite; a program needn't handle non-finite values.
Results may differ from a plain program's by a relative error of at most 0.018.
Values may be sent and summed in bfloat16 or wider, within the bound.
A program may use at most 768 MiB of HBM per device.

v0:
```python
import math

import jax
import jax.numpy as jnp
import numpy as np
from jax import lax
from jax.sharding import PartitionSpec as P

D = 768
H = 12
HD = 64
NBKT = 32
MAXD = 128
E = 4
WIN = 1024
QB = 512
BLK = 128


EPSILON = 1e-06
NEG_LARGE = -1e30


def cut_along(array, dim, size):
    lengths = array.shape
    tiles = array.reshape(*lengths[:dim], size, lengths[dim] // size, *lengths[dim + 1 :])
    return jnp.moveaxis(tiles, dim, 0)


def sum_at_owner(array, axis, dim):
    size = lax.axis_size(axis)
    tiles = lax.all_to_all(cut_along(array, dim, size), axis, 0, 0, tiled=True)
    return jnp.sum(tiles.astype(jnp.float32), axis=0)


def side_by_side(arrays, axis, dim, along):
    widths = [a.shape[along] for a in arrays]
    both = jnp.concatenate(arrays, axis=along)
    result = sum_at_owner(both, axis, dim)
    return tuple(jnp.split(result, [sum(widths[:k]) for k in range(1, len(widths))], axis=along))


def bucket_numbers(window, buckets, far_distance):
    distance = np.arange(window)
    exact_part = buckets // 2
    safe_distance = np.maximum(distance, 1) * 1.0
    log_part = exact_part + np.floor(
        np.log(safe_distance / exact_part)
        / np.log(far_distance / exact_part)
        * (buckets - exact_part)
    ).astype(np.int32)
    log_part = np.minimum(log_part, buckets - 1)
    return np.where(distance < exact_part, distance, log_part).astype(np.int32)


def band_tables():
    key_span = QB + WIN
    distance = np.arange(QB)[:, None] + WIN - np.arange(key_span)[None, :]
    in_band = (distance >= 0) & (distance < WIN)
    clipped = np.clip(distance, 0, WIN - 1)
    bucket_list = bucket_numbers(WIN, NBKT, MAXD)
    return (in_band, bucket_list[clipped], bucket_list)


def rms_apply(values, gain_vec):
    inverse = lax.rsqrt(jnp.mean(values * values, axis=-1, keepdims=True) + EPSILON)
    return values * inverse * gain_vec


def gelu_tanh(values):
    return jax.nn.gelu(values, approximate=True)


def diagonal_sums(block_values):
    heads_here, rows_here, span_here = block_values.shape
    flat = jnp.pad(
        block_values.reshape(heads_here, rows_here * span_here), ((0, 0), (0, rows_here))
    )
    skewed = flat.reshape(heads_here, rows_here, span_here + 1)
    return jnp.sum(skewed[:, :, 1 : WIN + 1], axis=1)


def expert_slots(route_ids):
    length = route_ids.shape[0]
    chosen = (route_ids[:, None] == jnp.arange(E, dtype=jnp.int32)[None, :]).astype(jnp.int32)
    before = jnp.cumsum(chosen, axis=0) - chosen
    rank_in = jnp.sum(before * chosen, axis=1)
    counts = jnp.sum(chosen, axis=0)
    padded = (counts + BLK - 1) // BLK * BLK
    starts = jnp.cumsum(padded) - padded
    slot_of_token = jnp.sum(starts[None, :] * chosen, axis=1) + rank_in
    capacity = length + E * BLK
    token_of_slot = (
        jnp.full((capacity,), length, jnp.int32)
        .at[slot_of_token]
        .set(jnp.arange(length, dtype=jnp.int32))
    )
    block_first = jnp.arange(capacity // BLK, dtype=jnp.int32) * BLK
    ends = starts + padded
    block_expert = jnp.minimum(
        jnp.sum((block_first[:, None] >= ends[None, :]).astype(jnp.int32), axis=1), E - 1
    )
    return (slot_of_token, token_of_slot, block_expert)


def per_device(
    tokens,
    segments,
    routes,
    cotangent,
    gain_attn,
    w_query,
    w_key,
    w_value,
    w_output,
    rel_table,
    gain_ffn,
    w_router,
    w_inner,
    w_outer,
):
    part_index = lax.axis_index("tensor")
    rows_local = tokens.shape[0]
    seq_len = segments.shape[0]
    heads_local = w_query.shape[1] // HD
    width_local = heads_local * HD
    key_span = QB + WIN
    num_blocks = seq_len // QB
    score_scale = 1.0 / math.sqrt(HD)
    in_band, bucket_ids, bucket_list = band_tables()
    band_mask = jnp.asarray(in_band)
    query_full, key_full, value_full, output_full = (
        lax.all_gather(w_query, "dp", axis=0, tiled=True),
        lax.all_gather(w_key, "dp", axis=0, tiled=True),
        lax.all_gather(w_value, "dp", axis=0, tiled=True),
        lax.all_gather(w_output, "dp", axis=1, tiled=True),
    )
    inner_full, outer_full = (
        lax.all_gather(w_inner, "dp", axis=1, tiled=True),
        lax.all_gather(w_outer, "dp", axis=2, tiled=True),
    )
    table_local = lax.dynamic_slice_in_dim(
        rel_table.astype(jnp.float32), part_index * heads_local, heads_local, 1
    )
    table_heads = jnp.transpose(table_local)
    bias_block = table_heads[:, jnp.asarray(bucket_ids)]
    normed_attn, norm_one_pull = jax.vjp(rms_apply, tokens, gain_attn.astype(jnp.float32))
    attn_rows = lax.all_gather(normed_attn.astype(jnp.bfloat16), "tensor", axis=0, tiled=True)
    queries_t = jnp.einsum(
        "sd,dw->ws", attn_rows, query_full, preferred_element_type=jnp.float32
    ).astype(jnp.bfloat16)
    keys_t = jnp.einsum(
        "sd,dw->ws", attn_rows, key_full, preferred_element_type=jnp.float32
    ).astype(jnp.bfloat16)
    values_t = jnp.einsum(
        "sd,dw->ws", attn_rows, value_full, preferred_element_type=jnp.float32
    ).astype(jnp.bfloat16)
    keys_pad = jnp.pad(keys_t, ((0, 0), (WIN, 0)))
    values_pad = jnp.pad(values_t, ((0, 0), (WIN, 0)))
    segs_pad = jnp.pad(segments, (WIN, 0), constant_values=-1)

    def block_rows(block_index):
        row_start = block_index * QB
        query_rows = lax.dynamic_slice_in_dim(queries_t, row_start, QB, 1).reshape(
            heads_local, HD, QB
        )
        key_rows = lax.dynamic_slice_in_dim(keys_pad, row_start, key_span, 1).reshape(
            heads_local, HD, key_span
        )
        value_rows = lax.dynamic_slice_in_dim(values_pad, row_start, key_span, 1).reshape(
            heads_local, HD, key_span
        )
        seg_query = lax.dynamic_slice_in_dim(segments, row_start, QB, 0)
        seg_key = lax.dynamic_slice_in_dim(segs_pad, row_start, key_span, 0)
        allowed = ((seg_query[:, None] == seg_key[None, :]) & band_mask)[None]
        scores = (
            jnp.einsum("hdq,hdk->hqk", query_rows, key_rows, preferred_element_type=jnp.float32)
            * score_scale
            + bias_block
        )
        return (query_rows, key_rows, value_rows, allowed, scores)

    def forward_block(block_index):
        query_rows, key_rows, value_rows, allowed, scores = block_rows(block_index)
        masked = jnp.where(allowed, scores, NEG_LARGE)
        row_peak = jnp.max(masked, axis=-1, keepdims=True)
        exp_terms = jnp.where(allowed, jnp.exp(masked - row_peak), 0.0)
        row_total = jnp.sum(exp_terms, axis=-1, keepdims=True)
        weights_low = (exp_terms / row_total).astype(jnp.bfloat16)
        context_rows = jnp.einsum(
            "hqk,hdk->hdq", weights_low, value_rows, preferred_element_type=jnp.float32
        )
        return (
            context_rows.reshape(width_local, QB).astype(jnp.bfloat16),
            (row_peak + jnp.log(row_total))[..., 0],
        )

    context_blocks, log_totals = lax.map(forward_block, jnp.arange(num_blocks, dtype=jnp.int32))
    context_t = jnp.transpose(context_blocks, (1, 0, 2)).reshape(width_local, seq_len)
    attn_branch = lax.psum_scatter(
        jnp.einsum("ws,wd->sd", context_t, output_full, preferred_element_type=jnp.float32).astype(
            jnp.bfloat16
        ),
        "tensor",
        scatter_dimension=0,
        tiled=True,
    ).astype(jnp.float32)
    attended = tokens + attn_branch
    normed_ffn, norm_two_pull = jax.vjp(rms_apply, attended, gain_ffn.astype(jnp.float32))
    ffn_in = normed_ffn.astype(jnp.bfloat16)
    ffn_rows = lax.all_gather(ffn_in, "tensor", axis=0, tiled=True)
    slot_of_token, token_of_slot, block_expert = expert_slots(routes[:, 0])
    padded_rows = jnp.concatenate([ffn_rows, jnp.zeros((1, D), jnp.bfloat16)], axis=0)
    slot_rows = padded_rows[token_of_slot].reshape(-1, BLK, D)

    def expert_forward(inputs):
        rows_in, expert_id = inputs
        inner_act = jnp.dot(
            rows_in,
            lax.dynamic_index_in_dim(inner_full, expert_id, 0, False),
            preferred_element_type=jnp.float32,
        )
        active = gelu_tanh(inner_act).astype(jnp.bfloat16)
        return (
            jnp.dot(
                active,
                lax.dynamic_index_in_dim(outer_full, expert_id, 0, False),
                preferred_element_type=jnp.float32,
            ),
            inner_act,
        )

    slot_out, slot_inner = lax.map(expert_forward, (slot_rows, block_expert))
    token_terms = slot_out.reshape(-1, D)[slot_of_token]
    expert_out = lax.psum_scatter(
        token_terms.astype(jnp.bfloat16), "tensor", scatter_dimension=0, tiled=True
    ).astype(jnp.float32)
    local_routes = lax.dynamic_slice_in_dim(routes[:, 0], part_index * rows_local, rows_local, 0)
    route_mask = (local_routes[:, None] == jnp.arange(E, dtype=jnp.int32)[None, :]).astype(
        jnp.float32
    )

    def gate_of(normed_values, router_values):
        logits = jnp.dot(normed_values, router_values, precision=lax.Precision.HIGHEST)
        return jnp.sum(jax.nn.softmax(logits, axis=-1) * route_mask, axis=-1)

    gate_weight, gate_pull = jax.vjp(
        gate_of, ffn_in.astype(jnp.float32), w_router.astype(jnp.float32)
    )
    output = attended + gate_weight[:, None] * expert_out
    query_back, key_back, value_back, output_back, inner_back, outer_back = (
        lax.all_gather(w_query, "dp", axis=0, tiled=True),
        lax.all_gather(w_key, "dp", axis=0, tiled=True),
        lax.all_gather(w_value, "dp", axis=0, tiled=True),
        lax.all_gather(w_output, "dp", axis=1, tiled=True),
        lax.all_gather(w_inner, "dp", axis=1, tiled=True),
        lax.all_gather(w_outer, "dp", axis=2, tiled=True),
    )
    d_expert = (cotangent * gate_weight[:, None]).astype(jnp.bfloat16)
    d_gate = jnp.sum(cotangent * expert_out, axis=-1)
    d_expert_rows = lax.all_gather(d_expert, "tensor", axis=0, tiled=True)
    d_slot_rows = jnp.concatenate([d_expert_rows, jnp.zeros((1, D), jnp.bfloat16)], axis=0)[
        token_of_slot
    ].reshape(-1, BLK, D)
    hidden_local = inner_back.shape[2]

    def expert_backward(carried, inputs):
        grad_in_acc, grad_out_acc = carried
        rows_in, d_rows_out, inner_act, expert_id = inputs
        inner_weight = lax.dynamic_index_in_dim(inner_back, expert_id, 0, False)
        outer_weight = lax.dynamic_index_in_dim(outer_back, expert_id, 0, False)
        active = gelu_tanh(inner_act).astype(jnp.bfloat16)
        d_active = jnp.einsum(
            "bd,fd->bf", d_rows_out, outer_weight, preferred_element_type=jnp.float32
        )
        d_inner = jax.vjp(gelu_tanh, inner_act)[1](d_active)[0].astype(jnp.bfloat16)
        grad_out_piece = jnp.einsum(
            "bf,bd->fd", active, d_rows_out, preferred_element_type=jnp.float32
        )
        grad_in_piece = jnp.einsum(
            "bd,bf->df", rows_in, d_inner, preferred_element_type=jnp.float32
        )
        d_rows_in = jnp.einsum(
            "bf,df->bd", d_inner, inner_weight, preferred_element_type=jnp.float32
        )
        grad_in_acc = lax.dynamic_update_index_in_dim(
            grad_in_acc,
            lax.dynamic_index_in_dim(grad_in_acc, expert_id, 0, False) + grad_in_piece,
            expert_id,
            0,
        )
        grad_out_acc = lax.dynamic_update_index_in_dim(
            grad_out_acc,
            lax.dynamic_index_in_dim(grad_out_acc, expert_id, 0, False) + grad_out_piece,
            expert_id,
            0,
        )
        return ((grad_in_acc, grad_out_acc), d_rows_in)

    start_grads = (
        jnp.zeros((E, D, hidden_local), jnp.float32),
        jnp.zeros((E, hidden_local, D), jnp.float32),
    )
    (grad_inner_full, grad_outer_full), d_slots = lax.scan(
        expert_backward, start_grads, (slot_rows, d_slot_rows, slot_inner, block_expert)
    )
    d_token_terms = d_slots.reshape(-1, D)[slot_of_token]
    d_ffn_local = lax.psum_scatter(
        d_token_terms.astype(jnp.bfloat16), "tensor", scatter_dimension=0, tiled=True
    ).astype(jnp.float32)
    d_ffn_router, grad_router_local = gate_pull(d_gate)
    d_attended_norm, grad_gain_two = norm_two_pull(d_ffn_local + d_ffn_router)
    d_attended = cotangent + d_attended_norm
    d_branch_rows = lax.all_gather(d_attended.astype(jnp.bfloat16), "tensor", axis=0, tiled=True)
    grad_output_full = jnp.einsum(
        "ws,sd->wd", context_t, d_branch_rows, preferred_element_type=jnp.float32
    )
    d_context_t = jnp.einsum(
        "wd,sd->ws", output_back, d_branch_rows, preferred_element_type=jnp.float32
    ).astype(jnp.bfloat16)

    def backward_block(carried, block_index):
        d_keys_acc, d_values_acc, diag_acc = carried
        row_start = block_index * QB
        query_rows, key_rows, value_rows, allowed, scores = block_rows(block_index)
        log_rows = lax.dynamic_index_in_dim(log_totals, block_index, 0, False)
        probabilities = jnp.where(
            allowed, jnp.exp(jnp.where(allowed, scores, NEG_LARGE) - log_rows[..., None]), 0.0
        )
        weights_low = probabilities.astype(jnp.bfloat16)
        d_context_rows = lax.dynamic_slice_in_dim(d_context_t, row_start, QB, 1).reshape(
            heads_local, HD, QB
        )
        d_probs = jnp.einsum(
            "hdq,hdk->hqk", d_context_rows, value_rows, preferred_element_type=jnp.float32
        )
        d_value_rows = jnp.einsum(
            "hqk,hdq->hdk", weights_low, d_context_rows, preferred_element_type=jnp.float32
        )
        row_inner = jnp.sum(d_probs * probabilities, axis=-1, keepdims=True)
        d_scores = (probabilities * (d_probs - row_inner)).astype(jnp.bfloat16)
        d_query_rows = (
            jnp.einsum("hqk,hdk->hdq", d_scores, key_rows, preferred_element_type=jnp.float32)
            * score_scale
        )
        d_key_rows = (
            jnp.einsum("hqk,hdq->hdk", d_scores, query_rows, preferred_element_type=jnp.float32)
            * score_scale
        )
        d_keys_acc = lax.dynamic_update_slice_in_dim(
            d_keys_acc,
            lax.dynamic_slice_in_dim(d_keys_acc, row_start, key_span, 1)
            + d_key_rows.reshape(width_local, key_span),
            row_start,
            1,
        )
        d_values_acc = lax.dynamic_update_slice_in_dim(
            d_values_acc,
            lax.dynamic_slice_in_dim(d_values_acc, row_start, key_span, 1)
            + d_value_rows.reshape(width_local, key_span),
            row_start,
            1,
        )
        diag_acc = diag_acc + diagonal_sums(d_scores.astype(jnp.float32))
        return (
            (d_keys_acc, d_values_acc, diag_acc),
            d_query_rows.reshape(width_local, QB).astype(jnp.bfloat16),
        )

    start_attn = (
        jnp.zeros((width_local, seq_len + WIN), jnp.float32),
        jnp.zeros((width_local, seq_len + WIN), jnp.float32),
        jnp.zeros((heads_local, WIN), jnp.float32),
    )
    (d_keys_pad, d_values_pad, diag_acc), d_query_blocks = lax.scan(
        backward_block, start_attn, jnp.arange(num_blocks, dtype=jnp.int32)
    )
    d_queries_t = jnp.transpose(d_query_blocks, (1, 0, 2)).reshape(width_local, seq_len)
    d_keys_t = d_keys_pad[:, WIN:].astype(jnp.bfloat16)
    d_values_t = d_values_pad[:, WIN:].astype(jnp.bfloat16)
    grad_query_full = jnp.einsum(
        "sd,ws->dw", attn_rows, d_queries_t, preferred_element_type=jnp.float32
    )
    grad_key_full = jnp.einsum("sd,ws->dw", attn_rows, d_keys_t, preferred_element_type=jnp.float32)
    grad_value_full = jnp.einsum(
        "sd,ws->dw", attn_rows, d_values_t, preferred_element_type=jnp.float32
    )
    total_rows = jnp.einsum(
        "ws,dw->sd", d_queries_t, query_back, preferred_element_type=jnp.float32
    )
    total_rows = total_rows + jnp.einsum(
        "ws,dw->sd", d_keys_t, key_back, preferred_element_type=jnp.float32
    )
    d_attn_local = lax.psum_scatter(
        (
            total_rows
            + jnp.einsum("ws,dw->sd", d_values_t, value_back, preferred_element_type=jnp.float32)
        ).astype(jnp.bfloat16),
        "tensor",
        scatter_dimension=0,
        tiled=True,
    ).astype(jnp.float32)
    d_tokens_norm, grad_gain_one = norm_one_pull(d_attn_local)
    grad_tokens = d_attended + d_tokens_norm
    by_distance = jnp.flip(diag_acc, axis=1)
    bucket_onehot = jnp.asarray(
        (bucket_list[:, None] == np.arange(NBKT)[None, :]).astype(np.float32)
    )
    grad_table_local = jnp.dot(bucket_onehot.T, by_distance.T, precision=lax.Precision.HIGHEST)
    grad_table_full = lax.dynamic_update_slice_in_dim(
        jnp.zeros((NBKT, H), jnp.float32), grad_table_local, part_index * heads_local, 1
    )
    small_sums = lax.psum(
        (grad_gain_one, grad_gain_two, grad_router_local, grad_table_full), ("dp", "tensor")
    )
    attn_grads = (
        *side_by_side(
            (
                grad_query_full.astype(jnp.bfloat16),
                grad_key_full.astype(jnp.bfloat16),
                grad_value_full.astype(jnp.bfloat16),
            ),
            "dp",
            0,
            1,
        ),
        sum_at_owner(grad_output_full.astype(jnp.bfloat16), "dp", 1),
    )
    expert_grads = (
        lax.psum_scatter(grad_inner_full, "dp", scatter_dimension=1, tiled=True),
        lax.psum_scatter(grad_outer_full, "dp", scatter_dimension=2, tiled=True),
    )
    return (
        output,
        grad_tokens,
        small_sums[0],
        attn_grads[0],
        attn_grads[1],
        attn_grads[2],
        attn_grads[3],
        small_sums[3],
        small_sums[1],
        small_sums[2],
        expert_grads[0],
        expert_grads[1],
    )


def solution(mesh):
    in_specs = (
        P(("dp", "tensor"), None),
        P("dp"),
        P("dp", None),
        P(("dp", "tensor"), None),
        P(),
        P("dp", "tensor"),
        P("dp", "tensor"),
        P("dp", "tensor"),
        P("tensor", "dp"),
        P(),
        P(),
        P(),
        P(None, "dp", "tensor"),
        P(None, "tensor", "dp"),
    )
    out_specs = (
        P(("dp", "tensor"), None),
        P(("dp", "tensor"), None),
        P(),
        P("dp", "tensor"),
        P("dp", "tensor"),
        P("dp", "tensor"),
        P("tensor", "dp"),
        P(),
        P(),
        P(),
        P(None, "dp", "tensor"),
        P(None, "tensor", "dp"),
    )
    return jax.shard_map(
        per_device, mesh=mesh, in_specs=in_specs, out_specs=out_specs, check_vma=False
    )
```

profile of v0, /device:TPU:0, one launch (start us, length us, event | category | flops | bytes accessed | tf_op | source)
XLA Modules:
  0.0 4295.0 jit_solution(15405421436404212663)
XLA Ops:
  15.5 2595.8 %gather_fusion = f32[786432,3]{1,0:T(8,128)} fusion(f32[3,32]{0,1:T(8,128)S(1)} %copy.62, s32[786432]{0:T(1024)S(1)} %broadcast_clamp_fusion), kind=kCustom, calls=%fused_computation | custom fusion | bytes 22020096 | tf_op jit(solution)/shard_map/gather | solution.py:146
  2611.4 209.4 %copy.63 = f32[512,1536,3]{1,0,2:T(8,128)} copy(f32[512,1536,3]{2,1,0:T(8,128)} %bitcast.22) | data formatting | bytes 18874368 | tf_op jit(solution)/shard_map/gather | solution.py:146
  2821.5 32.9 all_gather.37
  2854.4 31.0 all_gather.39
  2885.4 31.1 all_gather.38
  2916.5 33.0 all_gather.40
  2954.5 31.1 while.63
  2991.5 28.8 reduce-scatter.7.cloned.1.call-done
  3050.3 75.6 %all-gather.13.cloned.1.call-done = bf16[4,768,768]{1,0,2:T(4,128)(2,1)} async-done(((bf16[4,768,96]{1,0,2:T(4,128)(2,1)}), bf16[4,768,768]{1,0,2:T(4,128)(2,1)}) %all-gather.13.cloned.1.call-update) | async-done | bytes 4718608 | tf_op jit(solution)/shard_map/all_gather | solution.py:140
  3134.4 71.8 %all-gather.11.cloned.1.call-done = bf16[4,768,768]{2,1,0:T(8,128)(2,1)} async-done(((bf16[4,96,768]{2,1,0:T(8,128)(2,1)}), bf16[4,768,768]{2,1,0:T(8,128)(2,1)}) %all-gather.11.cloned.1.call-update) | async-done | bytes 4718608 | tf_op jit(solution)/shard_map/all_gather | solution.py:139
  3208.8 88.1 %while.61 = (s32[]{:T(128)}, bf16[12,128,768]{2,1,0:T(8,128)(2,1)S(1)}, f32[12,128,768]{2,1,0:T(8,128)}, bf16[12,128,768]{2,1,0:T(8,128)(2,1)}, s32[12]{0:T(128)...) while((s32[]{:T(128)}, ...), condition=%wide.region_19.20_spmd, body=%wide.region_18.19_spmd.sunk | while | flops 302874624 | bytes 4130459 | solution.py:233
  3304.5 24.3 reduce-scatter.9.cloned.1.call-done
  3331.6 19.7 all-gather.15.cloned.1.call-done
  3367.4 302.5 %while.62 = (s32[]{:T(128)}, f32[4,768,768]{2,1,0:T(8,128)}, f32[4,768,768]{1,2,0:T(8,128)}, bf16[12,128,768]{2,1,0:T(8,128)(2,1)}, s32[12]{0:T(128)}, /*index=5...) while((s32[]{:T(128)}, f32[4,768,768]{2,1,0:T(8,128)}, ...), condition=%wide.region_22.23_spmd, body=%wide.region_21.22_spmd.sunk | while | flops 608010240 | bytes 56626428 | solution.py:304
  3677.9 28.2 reduce-scatter.11.cloned.1.call-done
  3711.0 19.8 all-gather.17.cloned.1.call-done
  3737.6 166.8 %while.64 = (s32[]{:T(128)}, f32[192,2048]{1,0:T(8,128)}, f32[192,2048]{1,0:T(8,128)}, f32[3,1024]{1,0:T(4,128)}, bf16[2,192,512]{2,1,0:T(8,128)(2,1)}, /*index=...) while((s32[]{:T(128)}, f32[192,2048]{1,0:T(8,128)}, ...), condition=%wide.region_30.31_spmd.clone.clone, body=%wide.region_27.30_spmd.sunk.clone.clone.sunk | while | flops 1541703168 | bytes 221206208 | solution.py:375
  3774.8 9.4 multiply_convert_fusion.5
  3803.5 11.4 reshape.517
  3878.1 11.4 reshape.517
  3944.2 38.2 all-to-all-done
  3984.6 43.4 %all-reduce.6 = (f32[768]{0:T(1024)}, f32[32,12]{0,1:T(8,128)}, f32[768]{0:T(1024)}, f32[768,4]{0,1:T(4,128)}) all-reduce(f32[768]{0:T(1024)S(1)} %get-tuple-element.610, f32[32,12]{0,1:T(8,128)S(1)} %dynamic_update_slice.55, f32[768]{0:T(1024)S(1)} %copy-done.73, ...), channel_id=1, replica_groups=mesh['dp'=8,'tensor'=4] {'dp','tensor'}, use_global_device_ids=true, to_apply=%region_34.35 | all-reduce | flops 4992 | bytes 39936 | tf_op jit(solution)/shard_map/psum | solution.py:413
  4030.1 91.1 %reduce-scatter.15.cloned.1.call-done = f32[4,96,768]{2,1,0:T(8,128)} async-done(((f32[4,768,768]{2,1,0:T(8,128)}), f32[4,96,768]{2,1,0:T(8,128)}) %reduce-scatter.15.cloned.1.call-update) | async-done | bytes 1179664 | tf_op jit(solution)/shard_map/reduce_scatter | solution.py:430
  4121.2 166.6 %reduce-scatter.17.cloned.1.call-done = f32[4,768,96]{1,2,0:T(8,128)} async-done(((f32[4,768,768]{1,2,0:T(8,128)}), f32[4,768,96]{1,2,0:T(8,128)}) %reduce-scatter.17.cloned.1.call-update) | async-done | bytes 1179664 | tf_op jit(solution)/shard_map/reduce_scatter | solution.py:431
  (596 shorter events, 634.6 us)
Async XLA Ops:
  7.2 3296.0 %copy-start = (bf16[768,4]{0,1:T(4,128)(2,1)S(1)}, bf16[768,4]{0,1:T(4,128)(2,1)}, u32[]{:S(2)}) copy-start(bf16[768,4]{0,1:T(4,128)(2,1)} %param.36) | copy-start | bytes 18436
  7.2 2942.3 %all-gather.7.cloned.1.call-start = ((), (), s32[]{:S(2)}) async-start(), calls=%async_computation.8 | async-start | bytes 1966080 | tf_op jit(solution)/shard_map/all_gather | solution.py:148
  12.4 3007.9 %reduce-scatter.7.cloned.1.call-start = ((), (), s32[]{:S(2)}) async-start(), calls=%async_computation.9 | async-start | bytes 1966080 | tf_op jit(solution)/shard_map/reduce_scatter | solution.py:200
  2611.4 209.4 %copy-start.59 = (bf16[192,96]{1,0:T(8,128)(2,1)S(1)}, bf16[192,96]{1,0:T(8,128)(2,1)}, u32[]{:S(2)}) copy-start(bf16[192,96]{1,0:T(8,128)(2,1)} %param.33) | copy-start | bytes 110596
  2611.4 210.2 %copy-start.56 = (bf16[96,192]{1,0:T(8,128)(2,1)S(1)}, bf16[96,192]{1,0:T(8,128)(2,1)}, u32[]{:S(2)}) copy-start(bf16[96,192]{1,0:T(8,128)(2,1)} %param.32) | copy-start | bytes 110596
  2611.4 243.1 %copy-start.57 = (bf16[96,192]{1,0:T(8,128)(2,1)S(1)}, bf16[96,192]{1,0:T(8,128)(2,1)}, u32[]{:S(2)}) copy-start(bf16[96,192]{1,0:T(8,128)(2,1)} %param.31) | copy-start | bytes 110596
  2611.4 274.0 %copy-start.58 = (bf16[96,192]{1,0:T(8,128)(2,1)S(1)}, bf16[96,192]{1,0:T(8,128)(2,1)}, u32[]{:S(2)}) copy-start(bf16[96,192]{1,0:T(8,128)(2,1)} %param.30) | copy-start | bytes 110596
  2854.4 95.0 %copy-start.26 = (bf16[768,192]{1,0:T(8,128)(2,1)}, bf16[768,192]{1,0:T(8,128)(2,1)S(1)}, u32[]{:S(2)}) copy-start(bf16[768,192]{1,0:T(8,128)(2,1)S(1)} %all_gather.37) | copy-start | bytes 884740
  2885.4 66.4 %copy-start.28 = (bf16[768,192]{1,0:T(8,128)(2,1)}, bf16[768,192]{1,0:T(8,128)(2,1)S(1)}, u32[]{:S(2)}) copy-start(bf16[768,192]{1,0:T(8,128)(2,1)S(1)} %all_gather.39) | copy-start | bytes 884740
  2990.7 52.4 %all-gather.9.cloned.1.call-start = ((), (), s32[]{:S(2)}) async-start(), calls=%async_computation.10 | async-start | bytes 1966080 | tf_op jit(solution)/shard_map/all_gather | solution.py:211
  3023.3 102.6 %all-gather.13.cloned.1.call-start = ((), (), s32[]{:S(2)}) async-start(), calls=%async_computation.12 | async-start | bytes 5308416 | tf_op jit(solution)/shard_map/all_gather | solution.py:140
  3024.7 181.5 %all-gather.11.cloned.1.call-start = ((), (), s32[]{:S(2)}) async-start(), calls=%async_computation.11 | async-start | bytes 5308416 | tf_op jit(solution)/shard_map/all_gather | solution.py:139
  3025.3 303.6 %reduce-scatter.9.cloned.1.call-start = ((), (), s32[]{:S(2)}) async-start(), calls=%async_computation.13 | async-start | bytes 1966080 | tf_op jit(solution)/shard_map/reduce_scatter | solution.py:235
  3302.3 48.9 %all-gather.15.cloned.1.call-start = ((), (), s32[]{:S(2)}) async-start(), calls=%async_computation.14 | async-start | bytes 1966080 | tf_op jit(solution)/shard_map/all_gather | solution.py:261
  3331.5 374.6 %reduce-scatter.11.cloned.1.call-start = ((), (), s32[]{:S(2)}) async-start(), calls=%async_computation.15 | async-start | bytes 1966080 | tf_op jit(solution)/shard_map/reduce_scatter | solution.py:308
  3677.9 52.9 %all-gather.17.cloned.1.call-start = ((), (), s32[]{:S(2)}) async-start(), calls=%async_computation.16 | async-start | bytes 1966080 | tf_op jit(solution)/shard_map/all_gather | solution.py:314
  3710.9 272.4 %reduce-scatter.13.cloned.1.call-start = ((), (), s32[]{:S(2)}) async-start(), calls=%async_computation.17 | async-start | bytes 1966080 | tf_op jit(solution)/shard_map/reduce_scatter | solution.py:394
  3910.8 210.4 %reduce-scatter.15.cloned.1.call-start = ((), (), s32[]{:S(2)}) async-start(), calls=%async_computation.18 | async-start | bytes 10616832 | tf_op jit(solution)/shard_map/reduce_scatter | solution.py:430
  3911.5 376.3 %reduce-scatter.17.cloned.1.call-start = ((), (), s32[]{:S(2)}) async-start(), calls=%async_computation.19 | async-start | bytes 10616832 | tf_op jit(solution)/shard_map/reduce_scatter | solution.py:431
  3919.4 17.7 all-to-all-start.1
  3937.0 46.3 %copy-start.75 = (f32[256]{0:T(256)S(1)}, f32[256]{0:T(256)}, u32[]{:S(2)}) copy-start(f32[256]{0:T(256)} %copy-done.74) | copy-start | bytes 3076
  3937.0 45.4 %all-to-all-start = ((bf16[8,96,576]{2,1,0:T(8,128)(2,1)}), bf16[8,96,576]{2,1,0:T(8,128)(2,1)S(1)}, u32[]{:S(2)}, u32[]{:S(2)}) async-start(bf16[8,96,576]{2,1,0:T(8,128)(2,1)} %bitcast.39), calls=%async_computation.4 | async-start | bytes 1966080 | tf_op jit(solution)/shard_map/all_to_all | solution.py:32
  3940.9 87.1 %copy-start.83 = (f32[256]{0:T(256)S(1)}, f32[256]{0:T(256)}, u32[]{:S(2)}) copy-start(f32[256]{0:T(256)} %copy-done.82) | copy-start | bytes 3076
  3940.9 87.1 %copy-start.36 = (f32[256,768]{1,0:T(8,128)S(1)}, f32[256,768]{1,0:T(8,128)}, u32[]{:S(2)}) copy-start(f32[256,768]{1,0:T(8,128)} %get-tuple-element.703) | copy-start | bytes 2359300
  (114 other events, 1269.1 us)
Sparse Core Ops, SparseCore 0:
  12.5 22.3 all-gather.6
  2990.8 29.4 reduce-scatter.6
  3023.4 19.6 all-gather.8
  3045.9 79.8 all-gather.12
  3128.1 78.0 all-gather.10
  3302.5 26.3 reduce-scatter.8
  3331.6 19.6 all-gather.14
  3678.0 28.0 reduce-scatter.10
  3711.0 19.6 all-gather.16
  3910.9 28.1 reduce-scatter.12
  3943.3 177.8 reduce-scatter.14
  4125.2 162.5 reduce-scatter.16
where the time goes:
time: 4310 us; the launch traced here: 4300 us
  local copies, waits for them, and re-layouts  3130 us (73%)
  waiting for transfers between devices  582 us (14%)
  matrix products  251 us (6%)
  blocking collectives  171 us (4%)
  loops' own time  72.2 us (2%)
  other arithmetic  58.3 us (1%)
    gather x2, local copies, waits for them, and re-layouts, per_device(): bias_block = table_heads[:, jnp.asarray(bucket_ids)]  2810 us
    reduce_scatter x1, waiting for transfers between devices, per_device(): lax.psum_scatter(grad_outer_full, 'dp', scatter_dimension=2, tiled=True)  167 us
    reduce_scatter x1, waiting for transfers between devices, per_device(): lax.psum_scatter(grad_inner_full, 'dp', scatter_dimension=1, tiled=True)  91.1 us
  transfers between devices with their start and end apart: 14, of which 12 were waited for; matrix products, arithmetic and copies ran while one was open for 66% of the time, Pallas kernels for 0%

commit v1 on v0

v1 whole, which is shorter than its diff:
```python
import functools
import math

import jax
import jax.numpy as jnp
import numpy as np
from jax import lax
from jax.experimental import pallas as pl
from jax.experimental.pallas import tpu as pltpu
from jax.sharding import PartitionSpec as P

HD = 64
NBKT = 32
MAXD = 128
E = 4
WIN = 1024
QT = 256
HALF = 128
ROWS = 256

EPSILON = 1e-06
NEG_LARGE = -1e30
BF = jnp.bfloat16
F32 = jnp.float32
VMEM_MAX = 56 * 1024 * 1024


def bucket_numbers(window, buckets, far_distance):
    distance = np.arange(window)
    exact_part = buckets // 2
    safe_distance = np.maximum(distance, 1) * 1.0
    log_part = exact_part + np.floor(
        np.log(safe_distance / exact_part)
        / np.log(far_distance / exact_part)
        * (buckets - exact_part)
    ).astype(np.int32)
    log_part = np.minimum(log_part, buckets - 1)
    return np.where(distance < exact_part, distance, log_part).astype(np.int32)


BUCKETS = bucket_numbers(WIN, NBKT, MAXD)
FIRST = [int(np.argmax(BUCKETS == b)) for b in range(NBKT)]
NEAR = FIRST[NBKT - 1]


def nn(a, b):
    return lax.dot_general(a, b, (((1,), (0,)), ((), ())), preferred_element_type=F32)


def nt(a, b):
    return lax.dot_general(a, b, (((1,), (1,)), ((), ())), preferred_element_type=F32)


def tn(a, b):
    return lax.dot_general(a, b, (((0,), (0,)), ((), ())), preferred_element_type=F32)


def iota(shape, dim):
    return lax.broadcasted_iota(jnp.int32, shape, dim)


def gather_dp(shard, size):
    rows = shard.shape[0]
    if size != 8:
        return [lax.all_gather(shard, "dp", axis=0, tiled=True)], jnp.zeros((1,), jnp.int32)
    me = lax.axis_index("dp")
    z, y = me // 2, me % 2
    own = [shard] + [lax.ppermute(shard, "dp", z_shift(k)) for k in (1, 2, 3)]
    far = [lax.ppermute(piece, "dp", Y_SWAP) for piece in own]
    ids = [((z + 4 - k) % 4) * 2 + y for k in range(4)]
    ids += [((z + 4 - k) % 4) * 2 + 1 - y for k in range(4)]
    return own + far, (jnp.stack(ids) * rows).astype(jnp.int32)


Y_SWAP = [(d, d ^ 1) for d in range(8)]


def z_shift(k):
    return [(z * 2 + y, ((z + k) % 4) * 2 + y) for z in range(4) for y in range(2)]


def send_offsets(rows, size):
    if size != 8:
        return jnp.zeros((1,), jnp.int32)
    me = lax.axis_index("dp")
    z, y = me // 2, me % 2
    ids = [((z + k) % 4) * 2 + y for k in range(4)] + [((z + k) % 4) * 2 + 1 - y for k in range(4)]
    return (jnp.stack(ids) * rows).astype(jnp.int32)


def reduce_dp(parts, size):
    if size != 8:
        return lax.psum_scatter(parts[0][0], "dp", scatter_dimension=0, tiled=True).astype(F32)
    mine, other = parts
    got = lax.ppermute(other, "dp", Y_SWAP)
    total = mine[0].astype(F32) + got[0].astype(F32)
    arrived = []
    for k in (1, 2, 3):
        pair = (mine[k].astype(F32) + got[k].astype(F32)).astype(BF)
        arrived.append(lax.ppermute(pair, "dp", z_shift(k)))
    for piece in arrived:
        total = total + piece.astype(F32)
    return total


def plan_kernel(route_ref, slot_row_ref, slot_col_ref, plan_ref):
    length = route_ref.shape[1]
    route = route_ref[...]
    chosen = jnp.where(iota((8, length), 0) == route, 1.0, 0.0).astype(F32)
    upper = jnp.where(iota((length, length), 0) < iota((length, length), 1), 1.0, 0.0)
    before = nn(chosen.astype(BF), upper.astype(BF))
    rank = jnp.sum(chosen * before, axis=0, keepdims=True)
    start = jnp.int32(0)
    base = jnp.zeros((1, length), F32)
    for e in range(E):
        here = route == e
        count = jnp.sum(jnp.where(here, 1, 0))
        tiles = (count + (ROWS - 1)) // ROWS
        plan_ref[e] = tiles
        plan_ref[E + e] = start
        base = base + jnp.where(here, start.astype(F32), 0.0)
        start = start + tiles * ROWS
    slots = jnp.broadcast_to(rank + base, (8, length))
    slot_row_ref[...] = slots.astype(jnp.int32)
    slot_col_ref[...] = jnp.transpose(slots).astype(jnp.int32)


def make_plan(route_row):
    length = route_row.shape[1]
    return pl.pallas_call(
        plan_kernel,
        out_shape=(
            jax.ShapeDtypeStruct((8, length), jnp.int32),
            jax.ShapeDtypeStruct((length, 8), jnp.int32),
            jax.ShapeDtypeStruct((2 * E,), jnp.int32),
        ),
        in_specs=[pl.BlockSpec(memory_space=pltpu.VMEM)],
        out_specs=(
            pl.BlockSpec(memory_space=pltpu.VMEM),
            pl.BlockSpec(memory_space=pltpu.VMEM),
            pl.BlockSpec(memory_space=pltpu.SMEM),
        ),
        compiler_params=pltpu.CompilerParams(vmem_limit_bytes=VMEM_MAX),
        name="route_plan",
    )(route_row)


def fill_bias(bias_ref, table_ref, heads):
    step = iota((HALF, HALF), 1) - iota((HALF, HALF), 0)
    for side in range(2):
        distance = step + side * HALF
        tiles = [jnp.full((HALF, HALF), table_ref[h, NBKT - 1], F32) for h in range(heads)]
        for b in reversed(range(NBKT - 1)):
            below = distance < FIRST[b + 1]
            tiles = [jnp.where(below, table_ref[h, b], tiles[h]) for h in range(heads)]
        for h in range(heads):
            bias_ref[h, side] = tiles[h]


def biased_scores(raw, gap, h, bias_ref, table_ref, first_key, key_start, query_block):
    far = table_ref[h, NBKT - 1]
    keys = key_start + iota((QT, QT), 0)
    if gap >= 2:
        return jnp.where(keys >= first_key, raw + far, NEG_LARGE)
    diag, near = bias_ref[h, 0], bias_ref[h, 1]
    const = jnp.full((HALF, HALF), far, F32)
    if gap == 1:
        tile = jnp.concatenate(
            [
                jnp.concatenate([const, const], axis=1),
                jnp.concatenate([near, const], axis=1),
            ],
            axis=0,
        )
        return jnp.where(keys >= first_key, raw + tile, NEG_LARGE)
    tile = jnp.concatenate(
        [jnp.concatenate([diag, near], axis=1), jnp.concatenate([const, diag], axis=1)], axis=0
    )
    causal = iota((QT, QT), 0) <= iota((QT, QT), 1)
    return jnp.where((keys >= first_key) & causal, raw + tile, NEG_LARGE)


def load_rows(pieces, offsets_ref, whole, sem):
    rows = pieces[0].shape[0]
    copies = []
    for k, piece in enumerate(pieces):
        at = pl.ds(pl.multiple_of(offsets_ref[k], rows), rows)
        copies.append(pltpu.make_async_copy(piece, whole.at[at], sem.at[k]))
    for copy in copies:
        copy.start()
    return copies


def attend_kernel(heads, pieces, offsets_ref, table_ref, x_ref, first_ref, *refs):
    piece_refs = refs[:pieces]
    qkv_ref, ctx_ref, lse_ref, branch_ref, w_out_ref = refs[pieces : pieces + 5]
    w_ref, q_t, v_t, kn, bias_ref, s_ref, ctx_t, sem = refs[pieces + 5 :]
    width = heads * HD
    seq = x_ref.shape[0]
    copies = load_rows(piece_refs, offsets_ref, w_ref, sem)
    fill_bias(bias_ref, table_ref, heads)
    for copy in copies:
        copy.wait()
    w_out_ref[...] = w_ref[...]
    qkv = nn(x_ref[...], w_ref[:, : 3 * width]).astype(BF)
    qkv_ref[...] = qkv
    q_t[...] = jnp.transpose(qkv[:, :width]) * jnp.asarray(1.0 / math.sqrt(HD), BF)
    v_t[...] = jnp.transpose(qkv[:, 2 * width :])
    for h in range(heads):
        kn[h] = qkv[:, width + h * HD : width + (h + 1) * HD]
    for i in range(seq // QT):
        cols = slice(i * QT, (i + 1) * QT)
        first_key = first_ref[:, cols]
        for h in range(heads):
            band = slice(h * HD, (h + 1) * HD)
            q_blk = q_t[band, cols]
            peak = None
            for j in range(i + 1):
                raw = nn(kn[h, j * QT : (j + 1) * QT], q_blk)
                s = biased_scores(raw, i - j, h, bias_ref, table_ref, first_key, j * QT, i)
                s_ref[h, j] = s
                top = jnp.max(s, axis=0, keepdims=True)
                peak = top if peak is None else jnp.maximum(peak, top)
            total = jnp.zeros((1, QT), F32)
            acc = jnp.zeros((HD, QT), F32)
            for j in range(i + 1):
                p = jnp.exp(s_ref[h, j] - peak)
                total = total + jnp.sum(p, axis=0, keepdims=True)
                acc = acc + nn(v_t[band, j * QT : (j + 1) * QT], p.astype(BF))
            ctx_t[band, cols] = (acc / total).astype(BF)
            lse_ref[h : h + 1, cols] = peak + jnp.log(total)
    ctx = jnp.transpose(ctx_t[...])
    ctx_ref[...] = ctx
    branch_ref[...] = nt(ctx, w_ref[:, 3 * width :]).astype(BF)


def attend(x, pieces, offsets, table, first_key, heads):
    seq, model = x.shape
    width = heads * HD
    n = len(pieces)
    vmem = pl.BlockSpec(memory_space=pltpu.VMEM)
    smem = pl.BlockSpec(memory_space=pltpu.SMEM)
    return pl.pallas_call(
        functools.partial(attend_kernel, heads, n),
        out_shape=(
            jax.ShapeDtypeStruct((seq, 3 * width), BF),
            jax.ShapeDtypeStruct((seq, width), BF),
            jax.ShapeDtypeStruct((8, seq), F32),
            jax.ShapeDtypeStruct((seq, model), BF),
            jax.ShapeDtypeStruct((model, 4 * width), BF),
        ),
        in_specs=[smem, smem, vmem, vmem] + [pl.BlockSpec(memory_space=pl.ANY)] * n,
        out_specs=(vmem,) * 5,
        scratch_shapes=[
            pltpu.VMEM((model, 4 * width), BF),
            pltpu.VMEM((width, seq), BF),
            pltpu.VMEM((width, seq), BF),
            pltpu.VMEM((heads, seq, HD), BF),
            pltpu.VMEM((heads, 2, HALF, HALF), F32),
            pltpu.VMEM((heads, seq // QT, QT, QT), F32),
            pltpu.VMEM((width, seq), BF),
            pltpu.SemaphoreType.DMA((n,)),
        ],
        compiler_params=pltpu.CompilerParams(vmem_limit_bytes=VMEM_MAX),
        cost_estimate=pl.CostEstimate(flops=4 * 10**9, bytes_accessed=10**7, transcendentals=2 * 10**6),
        name="attend",
    )(offsets, table, x, first_key, *pieces)


def attend_back_kernel(
    heads, blocks, offs_ref, table_ref, d_ref, w_ref, qkv_ref, ctx_ref, lse_ref, first_ref, x_ref,
    rows_ref, diag_ref, *refs
):
    grads = refs[: len(blocks)]
    q_t, k_t, dc_t, kn, vn, qn, dcn, bias_ref, dq_t, dqkv, near_ref, delta_ref, acc_ref = refs[len(blocks) :]
    width = heads * HD
    seq = d_ref.shape[0]
    scale = jnp.asarray(1.0 / math.sqrt(HD), BF)
    fill_bias(bias_ref, table_ref, heads)
    d_rows = d_ref[...]
    ctx = ctx_ref[...]
    dc = nn(d_rows, w_ref[:, 3 * width :]).astype(BF)
    acc_ref[:, 3 * width :] = tn(d_rows, ctx)
    dct = jnp.transpose(dc)
    dc_t[...] = dct
    qkv = qkv_ref[...]
    q_t[...] = jnp.transpose(qkv[:, :width]) * scale
    k_t[...] = jnp.transpose(qkv[:, width : 2 * width])
    product = dct.astype(F32) * jnp.transpose(ctx).astype(F32)
    for h in range(heads):
        band = slice(h * HD, (h + 1) * HD)
        qn[h] = qkv[:, band] * scale
        kn[h] = qkv[:, width + h * HD : width + (h + 1) * HD]
        vn[h] = qkv[:, 2 * width + h * HD : 2 * width + (h + 1) * HD]
        dcn[h] = dc[:, band]
        delta_ref[h : h + 1] = jnp.sum(product[band], axis=0, keepdims=True)
    dq_t[...] = jnp.zeros_like(dq_t)
    near_ref[...] = jnp.zeros_like(near_ref)
    for j in range(seq // QT):
        keys = slice(j * QT, (j + 1) * QT)
        for h in range(heads):
            band = slice(h * HD, (h + 1) * HD)
            dk = jnp.zeros((QT, HD), F32)
            dv = jnp.zeros((QT, HD), F32)
            for i in range(j, seq // QT):
                cols = slice(i * QT, (i + 1) * QT)
                raw = nn(kn[h, keys], q_t[band, cols])
                s = biased_scores(raw, i - j, h, bias_ref, table_ref, first_ref[:, cols], j * QT, i)
                p = jnp.exp(s - lse_ref[h : h + 1, cols])
                dp = nn(vn[h, keys], dc_t[band, cols])
                ds = p * (dp - delta_ref[h : h + 1, cols])
                if i == j:
                    near_ref[h, 0] += ds[:HALF, :HALF] + ds[HALF:, HALF:]
                    near_ref[h, 1] += ds[:HALF, HALF:]
                elif i == j + 1:
                    near_ref[h, 1] += ds[HALF:, :HALF]
                ds = ds.astype(BF)
                dv = dv + nn(p.astype(BF), dcn[h, cols])
                dk = dk + nn(ds, qn[h, cols])
                dq_t[band, cols] += nn(k_t[band, keys], ds)
            dqkv[keys, width + h * HD : width + (h + 1) * HD] = dk.astype(BF)
            dqkv[keys, 2 * width + h * HD : 2 * width + (h + 1) * HD] = dv.astype(BF)
    dqkv[:, :width] = jnp.transpose((dq_t[...] * (1.0 / math.sqrt(HD))).astype(BF))
    d_qkv = dqkv[...]
    rows_ref[...] = nt(d_qkv, w_ref[:, : 3 * width]).astype(BF)
    acc_ref[:, : 3 * width] = tn(x_ref[...], d_qkv)
    scatter_rows(acc_ref, offs_ref, grads, blocks)
    key, query = iota((HALF, HALF), 0), iota((HALF, HALF), 1)
    lines = []
    for h in range(heads):
        both = near_ref[h, 0] + jnp.where(query < key, near_ref[h, 1], 0.0)
        for bit in range(7):
            turned = pltpu.roll(both, HALF - (1 << bit), 1)
            both = jnp.where((key >> bit) & 1 == 1, turned, both)
        lines.append(jnp.sum(both, axis=0, keepdims=True))
    lines += [jnp.zeros((8 - heads, HALF), F32)]
    diag_ref[...] = jnp.concatenate(lines, axis=0)


def scatter_rows(acc_ref, offs_ref, outs, blocks):
    k = 0
    for out, count in zip(outs, blocks):
        rows = out.shape[1]
        for b in range(count):
            at = pl.ds(pl.multiple_of(offs_ref[k], rows), rows)
            out[b] = acc_ref[at, :].astype(BF)
            k += 1


def attend_back(d_rows, w, qkv, ctx, lse, first_key, x, table, offs, heads, size):
    seq, model = x.shape
    width = heads * HD
    vmem = pl.BlockSpec(memory_space=pltpu.VMEM)
    smem = pl.BlockSpec(memory_space=pltpu.SMEM)
    blocks = (4, 4) if size == 8 else (1,)
    rows = model // sum(blocks)
    out = pl.pallas_call(
        functools.partial(attend_back_kernel, heads, blocks),
        out_shape=(
            jax.ShapeDtypeStruct((seq, model), BF),
            jax.ShapeDtypeStruct((8, HALF), F32),
            *[jax.ShapeDtypeStruct((b, rows, 4 * width), BF) for b in blocks],
        ),
        in_specs=[smem, smem] + [vmem] * 7,
        out_specs=(vmem,) * (2 + len(blocks)),
        scratch_shapes=[
            pltpu.VMEM((width, seq), BF),
            pltpu.VMEM((width, seq), BF),
            pltpu.VMEM((width, seq), BF),
            pltpu.VMEM((heads, seq, HD), BF),
            pltpu.VMEM((heads, seq, HD), BF),
            pltpu.VMEM((heads, seq, HD), BF),
            pltpu.VMEM((heads, seq, HD), BF),
            pltpu.VMEM((heads, 2, HALF, HALF), F32),
            pltpu.VMEM((width, seq), F32),
            pltpu.VMEM((seq, 3 * width), BF),
            pltpu.VMEM((heads, 2, HALF, HALF), F32),
            pltpu.VMEM((8, seq), F32),
            pltpu.VMEM((model, 4 * width), F32),
        ],
        compiler_params=pltpu.CompilerParams(vmem_limit_bytes=VMEM_MAX),
        cost_estimate=pl.CostEstimate(flops=10**10, bytes_accessed=10**7, transcendentals=2 * 10**6),
        name="attend_back",
    )(offs, table, d_rows, w, qkv, ctx, lse, first_key, x)
    return out[0], out[1], out[2:]


def expert_kernel(e, pieces, blocks, plan_ref, offsets_ref, goffs_ref, xd_ref, row_ref, col_ref, *refs):
    model = xd_ref.shape[1] // 2
    has_terms = e > 0
    terms_in = refs[0] if has_terms else None
    refs = refs[1:] if has_terms else refs
    piece_refs = refs[:pieces]
    terms_ref = refs[pieces]
    grads = refs[pieces + 1 : pieces + 1 + len(blocks)]
    w_ref, acc_ref, sem = refs[pieces + 1 + len(blocks) :]
    hidden = w_ref.shape[1] // 2
    length = xd_ref.shape[0]
    copies = load_rows(piece_refs, offsets_ref, w_ref, sem)
    if has_terms:
        terms_ref[...] = terms_in[...]
    else:
        terms_ref[...] = jnp.zeros_like(terms_ref)
    acc_ref[...] = jnp.zeros_like(acc_ref)
    for copy in copies:
        copy.wait()
    tiles = plan_ref[e]
    base = plan_ref[E + e]

    @pl.loop(0, tiles)
    def _(t):
        start = base + t * ROWS
        pick = jnp.where(row_ref[0:1, :] == start + iota((ROWS, length), 0), 1.0, 0.0).astype(BF)
        xd = nn(pick, xd_ref[...]).astype(BF)
        x, d = xd[:, :model], xd[:, model:]
        inner = nn(x, w_ref[:, :hidden])
        cubic = 0.044715 * inner * inner
        tanh = jnp.tanh(math.sqrt(2.0 / math.pi) * inner * (1.0 + cubic))
        half = 0.5 * (1.0 + tanh)
        active = (inner * half).astype(BF)
        slope = half + (0.5 * math.sqrt(2.0 / math.pi)) * inner * (1.0 - tanh * tanh) * (1.0 + 3.0 * cubic)
        out = nt(active, w_ref[:, hidden:]).astype(BF)
        d_inner = (nn(d, w_ref[:, hidden:]) * slope).astype(BF)
        acc_ref[:, :hidden] += tn(x, d_inner)
        acc_ref[:, hidden:] += tn(d, active)
        d_x = nt(d_inner, w_ref[:, :hidden]).astype(BF)
        place = jnp.where(col_ref[:, 0:1] == start + iota((length, ROWS), 1), 1.0, 0.0).astype(BF)
        terms_ref[:, :model] = (terms_ref[:, :model].astype(F32) + nn(place, out)).astype(BF)
        terms_ref[:, model:] = (terms_ref[:, model:].astype(F32) + nn(place, d_x)).astype(BF)

    scatter_rows(acc_ref, goffs_ref, grads, blocks)


def expert(e, plan, offsets, goffs, xd, slot_row, slot_col, terms, pieces, size):
    length, both = xd.shape
    model = both // 2
    hidden2 = pieces[0].shape[1]
    n = len(pieces)
    vmem = pl.BlockSpec(memory_space=pltpu.VMEM)
    smem = pl.BlockSpec(memory_space=pltpu.SMEM)
    blocks = (4, 4) if size == 8 else (1,)
    rows = model // sum(blocks)
    extra = [] if terms is None else [terms]
    out = pl.pallas_call(
        functools.partial(expert_kernel, e, n, blocks),
        out_shape=(
            jax.ShapeDtypeStruct((length, both), BF),
            *[jax.ShapeDtypeStruct((b, rows, hidden2), BF) for b in blocks],
        ),
        in_specs=[smem] * 3 + [vmem] * (3 + len(extra)) + [pl.BlockSpec(memory_space=pl.ANY)] * n,
        out_specs=(vmem,) * (1 + len(blocks)),
        scratch_shapes=[
            pltpu.VMEM((model, hidden2), BF),
            pltpu.VMEM((model, hidden2), F32),
            pltpu.SemaphoreType.DMA((n,)),
        ],
        compiler_params=pltpu.CompilerParams(vmem_limit_bytes=VMEM_MAX),
        cost_estimate=pl.CostEstimate(flops=3 * 10**9, bytes_accessed=10**7, transcendentals=10**6),
        name=f"expert_{e}",
    )(plan, offsets, goffs, xd, slot_row, slot_col, *extra, *pieces)
    return out[0], out[1:]


def rms_apply(values, gain_vec):
    inverse = lax.rsqrt(jnp.mean(values * values, axis=-1, keepdims=True) + EPSILON)
    return values * inverse * gain_vec


def per_device(
    sizes,
    tokens,
    segments,
    routes,
    cotangent,
    gain_attn,
    w_query,
    w_key,
    w_value,
    w_output,
    rel_table,
    gain_ffn,
    w_router,
    w_inner,
    w_outer,
):
    size = sizes["dp"]
    part_index = lax.axis_index("tensor")
    rows_local, model = tokens.shape
    seq_len = segments.shape[0]
    width = w_query.shape[1]
    heads = width // HD
    all_heads = rel_table.shape[1]
    hidden = w_inner.shape[2]
    shard_rows = w_query.shape[0]

    attn_shard = jnp.concatenate([w_query, w_key, w_value, jnp.transpose(w_output)], axis=1)
    attn_pieces, offsets = gather_dp(attn_shard, size)
    both_shard = jnp.concatenate([w_inner, jnp.transpose(w_outer, (0, 2, 1))], axis=2)
    expert_pieces = [gather_dp(both_shard[e], size)[0] for e in range(E)]
    goffs = send_offsets(shard_rows, size)

    route_row = jnp.reshape(routes, (1, seq_len))
    slot_row, slot_col, plan = make_plan(route_row)
    counts = [jnp.sum((segments < s).astype(jnp.int32)) for s in range(1, 5)]
    first_key = jnp.zeros_like(segments)
    for s in range(1, 5):
        first_key = jnp.where(segments >= s, counts[s - 1], first_key)
    first_key = first_key[None, :]
    table = jnp.transpose(
        lax.dynamic_slice_in_dim(rel_table.astype(F32), part_index * heads, heads, 1)
    )

    normed_attn, norm_one_pull = jax.vjp(rms_apply, tokens, gain_attn.astype(F32))
    attn_rows = lax.all_gather(normed_attn.astype(BF), "tensor", axis=0, tiled=True)
    qkv, ctx, lse, branch, w_attn = attend(attn_rows, attn_pieces, offsets, table, first_key, heads)
    attended = tokens + lax.psum_scatter(
        branch, "tensor", scatter_dimension=0, tiled=True
    ).astype(F32)

    normed_ffn, norm_two_pull = jax.vjp(rms_apply, attended, gain_ffn.astype(F32))
    ffn_in = normed_ffn.astype(BF)
    local_routes = lax.dynamic_slice_in_dim(routes[:, 0], part_index * rows_local, rows_local, 0)
    route_mask = (local_routes[:, None] == jnp.arange(E, dtype=jnp.int32)[None, :]).astype(F32)

    def gate_of(normed_values, router_values):
        logits = jnp.dot(normed_values, router_values, precision=lax.Precision.HIGHEST)
        return jnp.sum(jax.nn.softmax(logits, axis=-1) * route_mask, axis=-1)

    gate_weight, gate_pull = jax.vjp(gate_of, ffn_in.astype(F32), w_router.astype(F32))
    d_expert = (cotangent * gate_weight[:, None]).astype(BF)
    xd = lax.all_gather(
        jnp.concatenate([ffn_in, d_expert], axis=1), "tensor", axis=0, tiled=True
    )

    terms = None
    expert_sums = []
    for e in range(E):
        terms, parts = expert(
            e, plan, offsets, goffs, xd, slot_row, slot_col, terms, expert_pieces[e], size
        )
        expert_sums.append(reduce_dp(parts, size))
    sums = lax.psum_scatter(terms, "tensor", scatter_dimension=0, tiled=True).astype(F32)
    expert_out, d_ffn_local = sums[:, :model], sums[:, model:]
    output = attended + gate_weight[:, None] * expert_out
    d_gate = jnp.sum(cotangent * expert_out, axis=-1)

    d_ffn_router, grad_router_local = gate_pull(d_gate)
    d_attended_norm, grad_gain_two = norm_two_pull(d_ffn_local + d_ffn_router)
    d_attended = cotangent + d_attended_norm
    d_branch_rows = lax.all_gather(d_attended.astype(BF), "tensor", axis=0, tiled=True)

    total_rows, diag, attn_parts = attend_back(
        d_branch_rows, w_attn, qkv, ctx, lse, first_key, attn_rows, table, goffs, heads, size
    )
    attn_sum = reduce_dp(attn_parts, size)
    d_attn_local = lax.psum_scatter(
        total_rows, "tensor", scatter_dimension=0, tiled=True
    ).astype(F32)
    d_tokens_norm, grad_gain_one = norm_one_pull(d_attn_local)
    grad_tokens = d_attended + d_tokens_norm

    onehot = jnp.asarray((BUCKETS[:HALF, None] == np.arange(NBKT - 1)[None, :]).astype(np.float32))
    near_sums = jnp.dot(onehot.T, diag[:heads].T, precision=lax.Precision.HIGHEST)
    table_local = jnp.concatenate([near_sums, -jnp.sum(near_sums, axis=0, keepdims=True)], axis=0)
    grad_table_full = lax.dynamic_update_slice_in_dim(
        jnp.zeros((NBKT, all_heads), F32), table_local, part_index * heads, 1
    )
    small_sums = lax.psum(
        (grad_gain_one, grad_gain_two, grad_router_local, grad_table_full), ("dp", "tensor")
    )
    grad_inner = jnp.stack([s[:, :hidden] for s in expert_sums])
    grad_outer = jnp.stack([jnp.transpose(s[:, hidden:]) for s in expert_sums])
    return (
        output,
        grad_tokens,
        small_sums[0],
        attn_sum[:, :width],
        attn_sum[:, width : 2 * width],
        attn_sum[:, 2 * width : 3 * width],
        jnp.transpose(attn_sum[:, 3 * width :]),
        small_sums[3],
        small_sums[1],
        small_sums[2],
        grad_inner,
        grad_outer,
    )


def solution(mesh):
    sizes = dict(mesh.shape)
    in_specs = (
        P(("dp", "tensor"), None),
        P("dp"),
        P("dp", None),
        P(("dp", "tensor"), None),
        P(),
        P("dp", "tensor"),
        P("dp", "tensor"),
        P("dp", "tensor"),
        P("tensor", "dp"),
        P(),
        P(),
        P(),
        P(None, "dp", "tensor"),
        P(None, "tensor", "dp"),
    )
    out_specs = (
        P(("dp", "tensor"), None),
        P(("dp", "tensor"), None),
        P(),
        P("dp", "tensor"),
        P("dp", "tensor"),
        P("dp", "tensor"),
        P("tensor", "dp"),
        P(),
        P(),
        P(),
        P(None, "dp", "tensor"),
        P(None, "tensor", "dp"),
    )
    return jax.shard_map(
        functools.partial(per_device, sizes),
        mesh=mesh,
        in_specs=in_specs,
        out_specs=out_specs,
        check_vma=False,
    )
```

time: 4310 us -> 545 us (0.13)
  local copies, waits for them, and re-layouts: 3130 us -> 10.7 us
  waiting for transfers between devices: 582 us -> 193 us
  matrix products: 251 us -> 2.17 us
  starting transfers between devices: 9.77 us -> 157 us
  blocking collectives: 171 us -> 42.2 us
  Pallas kernels: 0 us -> 80.1 us
  loops' own time: 72.2 us -> 0 us
    gather x6 -> x0, local copies, waits for them, and re-layouts: 2830 us -> none  [the longest x2 2810 us: per_device(): bias_block = table_heads[:, jnp.asarray(bucket_ids)]]
    reduce_scatter x6 -> x3, waiting for transfers between devices: 339 us -> 28.4 us  [the longest x1 28.4 us: per_device(): lax.psum_scatter(branch, 'tensor', scatter_dimension=0, tiled=True)]
    dot_general x99 -> x1, matrix products: 247 us -> 0.29 us  [per_device(): jnp.dot(onehot.T, diag[:heads].T, precision=lax.Precision.HIGHEST)]
    all_gather x6 -> x3, waiting for transfers between devices: 195 us -> 0.01 us  [the longest x1 0.01 us: per_device(): lax.all_gather(normed_attn.astype(BF), 'tensor', axis=0, tiled=True)]
    ppermute x0 -> x55, waiting for transfers between devices: none -> 164 us  [the longest x5 78.7 us: reduce_dp(): got = lax.ppermute(other, 'dp', Y_SWAP)]
    ppermute x0 -> x55, starting transfers between devices: none -> 157 us  [the longest x15 63.5 us: gather_dp(): own = [shard] + [lax.ppermute(shard, 'dp', z_shift(k)) for k in (1, 2, 3)]]
    all_gather x4 -> x0, blocking collectives: 128 us -> none  [the longest x1 33 us: per_device(): lax.all_gather(w_output, 'dp', axis=1, tiled=True)]
    dynamic_slice x84 -> x0, local copies, waits for them, and re-layouts: 126 us -> none  [the longest x24 63.4 us: expert_backward(): lax.dynamic_index_in_dim(grad_out_acc, expert_id, 0, False) + grad_out_piece]
  transfers between devices with their start and end apart: 14 -> 61, of which waited for: 12 -> 23; matrix products, arithmetic and copies ran while one was open for 66% -> 6% of each run, Pallas kernels for 0% -> 11%
where the time goes in v1:
time: 545 us; the launch traced here: 538 us
  waiting for transfers between devices  193 us (35%)
  starting transfers between devices  157 us (29%)
  Pallas kernels  80.1 us (15%)
  blocking collectives  42.2 us (8%)
  other arithmetic  37.7 us (7%)
  between operations  15.2 us (3%)
  local copies, waits for them, and re-layouts  10.7 us (2%)
    ppermute x5, waiting for transfers between devices, reduce_dp(): got = lax.ppermute(other, 'dp', Y_SWAP)  78.7 us
    ppermute x15, starting transfers between devices, gather_dp(): own = [shard] + [lax.ppermute(shard, 'dp', z_shift(k)) for k in (1, 2, 3)]  63.5 us
    ppermute x15, starting transfers between devices, reduce_dp(): arrived.append(lax.ppermute(pair, 'dp', z_shift(k)))  62.1 us
    pallas_call x4, Pallas kernels, expert(): pl.pallas_call(functools.partial(expert_kernel, e, n, blocks), out_shape=...  52.1 us
    psum x1, blocking collectives, per_device(): lax.psum((grad_gain_one, grad_gain_two, grad_router_local, grad_table_ful...  42.2 us
    ppermute x15, waiting for transfers between devices, gather_dp(): own = [shard] + [lax.ppermute(shard, 'dp', z_shift(k)) for k in (1, 2, 3)]  36 us
    reduce_scatter x1, waiting for transfers between devices, per_device(): lax.psum_scatter(branch, 'tensor', scatter_dimension=0, tiled=True)  28.4 us
    ppermute x15, waiting for transfers between devices, reduce_dp(): arrived.append(lax.ppermute(pair, 'dp', z_shift(k)))  26.2 us
  transfers between devices with their start and end apart: 61, of which 23 were waited for; matrix products, arithmetic and copies ran while one was open for 6% of the time, Pallas kernels for 11%

profile of v1, /device:TPU:0, one launch (start us, length us, event | category | flops | bytes accessed | tf_op | source)
XLA Modules:
  0.0 538.0 jit_solution(16899232658837805672)
XLA Ops:
  35.4 11.0 %attend.1 = (bf16[1024,576]{1,0:T(8,128)(2,1)}, bf16[1024,192]{1,0:T(8,128)(2,1)}, f32[8,1024]{1,0:T(8,128)}, bf16[1024,768]{1,0:T(8,128)(2,1)}, bf16[768,768]{1,0:T(8,128)(2,1)}) custom-call(s32[8]{0:T(128)} %broadcast_multiply_fusion.1.offsets_ref, f32[3,32]{1,0:T(4,128)} %convert_bitcast_fusion.table_ref, ...), custom_call_target="tpu_custom_call" | custom-call | flops 4000000000 | bytes 10000000 | tf_op jit(solution)/shard_map/attend/pallas_call | solution.py:243
  47.9 28.4 %reduce-scatter.4.cloned.1.call-done = bf16[256,768]{1,0:T(8,128)(2,1)} async-done(((bf16[1024,768]{1,0:T(8,128)(2,1)}), bf16[256,768]{1,0:T(8,128)(2,1)}) %reduce-scatter.4.cloned.1.call-update) | async-done | bytes 393232 | tf_op jit(solution)/shard_map/reduce_scatter | solution.py:516
  93.9 13.1 %collective-permute-start.15 = (bf16[96,1536]{1,0:T(8,128)(2,1)S(1)}, bf16[96,1536]{1,0:T(8,128)(2,1)S(1)}, u32[]{:S(2)}, u32[]{:S(2)}) collective-permute-start(bf16[96,1536]{1,0:T(8,128)(2,1)S(1)} %get-tuple-element.107.refs_1_), channel_id=1, source_target_pairs={{0,16},{4,20},{8,24},{12,28},{16,0},{20,4},{24,8},{28,12},{1,17},{... | collective-permute-start | bytes 884744 | tf_op jit(solution)/shard_map/ppermute | solution.py:68
  107.0 16.7 %collective-permute-start.16 = (bf16[96,1536]{1,0:T(8,128)(2,1)S(1)}, bf16[96,1536]{1,0:T(8,128)(2,1)S(1)}, u32[]{:S(2)}, u32[]{:S(2)}) collective-permute-start(bf16[96,1536]{1,0:T(8,128)(2,1)S(1)} %get-tuple-element.107.refs_1_), channel_id=1, source_target_pairs={{0,24},{4,28},{8,0},{12,4},{16,8},{20,12},{24,16},{28,20},{1,25},{... | collective-permute-start | bytes 884744 | tf_op jit(solution)/shard_map/ppermute | solution.py:68
  132.2 11.0 %collective-permute-done.15.refs_3_ = bf16[96,1536]{1,0:T(8,128)(2,1)S(1)} collective-permute-done((bf16[96,1536]{1,0:T(8,128)(2,1)S(1)}, bf16[96,1536]{1,0:T(8,128)(2,1)S(1)}, u32[]{:S(2)}, u32[]{:S(2)}) %collective-permute-start.15) | collective-permute-done | bytes 294944 | tf_op jit(solution)/shard_map/ppermute | solution.py:68
  145.5 6.8 %collective-permute-start.28 = (bf16[96,1536]{1,0:T(8,128)(2,1)}, bf16[96,1536]{1,0:T(8,128)(2,1)S(1)}, u32[]{:S(2)}, u32[]{:S(2)}) collective-permute-start(bf16[96,1536]{1,0:T(8,128)(2,1)} %get-tuple-element.105.refs_1_), channel_id=1, source_target_pairs={{0,8},{4,12},{8,16},{12,20},{16,24},{20,28},{24,0},{28,4},{1,9},{5... | collective-permute-start | bytes 884744 | tf_op jit(solution)/shard_map/ppermute | solution.py:68
  157.5 11.1 %collective-permute-done.22.refs_3_ = bf16[96,1536]{1,0:T(8,128)(2,1)S(1)} collective-permute-done((bf16[96,1536]{1,0:T(8,128)(2,1)S(1)}, bf16[96,1536]{1,0:T(8,128)(2,1)S(1)}, u32[]{:S(2)}, u32[]{:S(2)}) %collective-permute-start.22) | collective-permute-done | bytes 294944 | tf_op jit(solution)/shard_map/ppermute | solution.py:68
  174.8 6.5 %collective-permute-done.29.refs_3_ = bf16[96,1536]{1,0:T(8,128)(2,1)S(1)} collective-permute-done((bf16[96,1536]{1,0:T(8,128)(2,1)}, bf16[96,1536]{1,0:T(8,128)(2,1)S(1)}, u32[]{:S(2)}, u32[]{:S(2)}) %collective-permute-start.29) | collective-permute-done | bytes 294944 | tf_op jit(solution)/shard_map/ppermute | solution.py:68
  201.8 10.5 %expert_0.1 = (bf16[1024,1536]{1,0:T(8,128)(2,1)}, bf16[4,96,1536]{2,1,0:T(8,128)(2,1)}, bf16[4,96,1536]{2,1,0:T(8,128)(2,1)}) custom-call(s32[8]{0:T(128)} %get-tuple-element.37.plan_ref, s32[8]{0:T(128)} %broadcast_multiply_fusion.1.offsets_ref, s32[8]{0:T(128)} %broadcast_multiply_fusion.goffs_ref.offs_ref, ...), custom_call_target="tpu_custom_call" | custom-call | flops 3000000000 | bytes 10000000 | tf_op jit(solution)/shard_map/expert_0/pallas_call | solution.py:444
  227.1 14.9 %expert_1.1 = (bf16[1024,1536]{1,0:T(8,128)(2,1)}, bf16[4,96,1536]{2,1,0:T(8,128)(2,1)}, bf16[4,96,1536]{2,1,0:T(8,128)(2,1)}) custom-call(s32[8]{0:T(128)} %get-tuple-element.37.plan_ref, s32[8]{0:T(128)} %broadcast_multiply_fusion.1.offsets_ref, s32[8]{0:T(128)} %broadcast_multiply_fusion.goffs_ref.offs_ref, ...), custom_call_target="tpu_custom_call" | custom-call | flops 3000000000 | bytes 10000000 | tf_op jit(solution)/shard_map/expert_1/pallas_call | solution.py:444
  242.0 15.6 %expert_2.1 = (bf16[1024,1536]{1,0:T(8,128)(2,1)}, bf16[4,96,1536]{2,1,0:T(8,128)(2,1)}, bf16[4,96,1536]{2,1,0:T(8,128)(2,1)}) custom-call(s32[8]{0:T(128)} %get-tuple-element.37.plan_ref, s32[8]{0:T(128)} %broadcast_multiply_fusion.1.offsets_ref, s32[8]{0:T(128)} %broadcast_multiply_fusion.goffs_ref.offs_ref, ...), custom_call_target="tpu_custom_call" | custom-call | flops 3000000000 | bytes 10000000 | tf_op jit(solution)/shard_map/expert_2/pallas_call | solution.py:444
  258.6 11.1 %expert_3.1 = (bf16[1024,1536]{1,0:T(8,128)(2,1)}, bf16[4,96,1536]{2,1,0:T(8,128)(2,1)}, bf16[4,96,1536]{2,1,0:T(8,128)(2,1)}) custom-call(s32[8]{0:T(128)} %get-tuple-element.37.plan_ref, s32[8]{0:T(128)} %broadcast_multiply_fusion.1.offsets_ref, s32[8]{0:T(128)} %broadcast_multiply_fusion.goffs_ref.offs_ref, ...), custom_call_target="tpu_custom_call" | custom-call | flops 3000000000 | bytes 10000000 | tf_op jit(solution)/shard_map/expert_3/pallas_call | solution.py:444
  274.0 25.1 %collective-permute-done.39 = bf16[4,96,1536]{2,1,0:T(8,128)(2,1)S(1)} collective-permute-done((bf16[4,96,1536]{2,1,0:T(8,128)(2,1)}, bf16[4,96,1536]{2,1,0:T(8,128)(2,1)S(1)}, u32[]{:S(2)}, u32[]{:S(2)}) %collective-permute-start.39) | collective-permute-done | bytes 1179680 | tf_op jit(solution)/shard_map/ppermute | solution.py:95
  307.4 16.9 %collective-permute-done.43 = bf16[4,96,1536]{2,1,0:T(8,128)(2,1)S(1)} collective-permute-done((bf16[4,96,1536]{2,1,0:T(8,128)(2,1)}, bf16[4,96,1536]{2,1,0:T(8,128)(2,1)S(1)}, u32[]{:S(2)}, u32[]{:S(2)}) %collective-permute-start.43) | collective-permute-done | bytes 1179680 | tf_op jit(solution)/shard_map/ppermute | solution.py:95
  332.0 17.7 %collective-permute-done.47 = bf16[4,96,1536]{2,1,0:T(8,128)(2,1)} collective-permute-done((bf16[4,96,1536]{2,1,0:T(8,128)(2,1)}, bf16[4,96,1536]{2,1,0:T(8,128)(2,1)}, u32[]{:S(2)}, u32[]{:S(2)}) %collective-permute-start.47) | collective-permute-done | bytes 1179680 | tf_op jit(solution)/shard_map/ppermute | solution.py:95
  349.7 5.7 %collective-permute-start.44 = (bf16[96,1536]{1,0:T(8,128)(2,1)}, bf16[96,1536]{1,0:T(8,128)(2,1)S(1)}, u32[]{:S(2)}, u32[]{:S(2)}) collective-permute-start(bf16[96,1536]{1,0:T(8,128)(2,1)} %get-tuple-element.91), channel_id=1, source_target_pairs={{0,8},{4,12},{8,16},{12,20},{16,24},{20,28},{24,0},{28,4},{1,9},{5... | collective-permute-start | bytes 884744 | tf_op jit(solution)/shard_map/ppermute | solution.py:100
  357.1 12.7 %collective-permute-done.51 = bf16[4,96,1536]{2,1,0:T(8,128)(2,1)} collective-permute-done((bf16[4,96,1536]{2,1,0:T(8,128)(2,1)}, bf16[4,96,1536]{2,1,0:T(8,128)(2,1)}, u32[]{:S(2)}, u32[]{:S(2)}) %collective-permute-start.51) | collective-permute-done | bytes 1179680 | tf_op jit(solution)/shard_map/ppermute | solution.py:95
  369.8 8.1 %collective-permute-start.45 = (bf16[96,1536]{1,0:T(8,128)(2,1)S(1)}, bf16[96,1536]{1,0:T(8,128)(2,1)S(1)}, u32[]{:S(2)}, u32[]{:S(2)}) collective-permute-start(bf16[96,1536]{1,0:T(8,128)(2,1)S(1)} %copy-done.17), channel_id=1, source_target_pairs={{0,16},{4,20},{8,24},{12,28},{16,0},{20,4},{24,8},{28,12},{1,17},{... | collective-permute-start | bytes 884744 | tf_op jit(solution)/shard_map/ppermute | solution.py:100
  398.7 13.2 %collective-permute-start.53 = (bf16[96,1536]{1,0:T(8,128)(2,1)}, bf16[96,1536]{1,0:T(8,128)(2,1)}, u32[]{:S(2)}, u32[]{:S(2)}) collective-permute-start(bf16[96,1536]{1,0:T(8,128)(2,1)} %get-tuple-element.99), channel_id=1, source_target_pairs={{0,16},{4,20},{8,24},{12,28},{16,0},{20,4},{24,8},{28,12},{1,17},{... | collective-permute-start | bytes 884744 | tf_op jit(solution)/shard_map/ppermute | solution.py:100
  417.1 13.0 %collective-permute-done.49 = bf16[96,1536]{1,0:T(8,128)(2,1)S(1)} collective-permute-done((bf16[96,1536]{1,0:T(8,128)(2,1)S(1)}, bf16[96,1536]{1,0:T(8,128)(2,1)S(1)}, u32[]{:S(2)}, u32[]{:S(2)}) %collective-permute-start.49) | collective-permute-done | bytes 294944 | tf_op jit(solution)/shard_map/ppermute | solution.py:100
  432.2 15.0 %attend_back.1 = (bf16[1024,768]{1,0:T(8,128)(2,1)}, f32[8,128]{1,0:T(8,128)}, bf16[4,96,768]{2,1,0:T(8,128)(2,1)}, bf16[4,96,768]{2,1,0:T(8,128)(2,1)}) custom-call(s32[8]{0:T(128)} %broadcast_multiply_fusion.goffs_ref.offs_ref, f32[3,32]{1,0:T(4,128)} %convert_bitcast_fusion.table_ref, bf16[1024,768]{1,0:T(8,128)(2,1)} %all-gather.8.cloned.1.call-done.d_ref, ...), custom_call_target="tpu_custom_call" | custom-call | flops 10000000000 | bytes 10000000 | tf_op jit(solution)/shard_map/attend_back/pallas_call | solution.py:357
  454.6 6.4 %collective-permute-done.35 = bf16[4,96,768]{2,1,0:T(8,128)(2,1)S(1)} collective-permute-done((bf16[4,96,768]{2,1,0:T(8,128)(2,1)S(1)}, bf16[4,96,768]{2,1,0:T(8,128)(2,1)S(1)}, u32[]{:S(2)}, u32[]{:S(2)}) %collective-permute-start.35) | collective-permute-done | bytes 589856 | tf_op jit(solution)/shard_map/ppermute | solution.py:95
  461.8 9.8 %collective-permute-start.36 = (bf16[96,768]{1,0:T(8,128)(2,1)S(1)}, bf16[96,768]{1,0:T(8,128)(2,1)S(1)}, u32[]{:S(2)}, u32[]{:S(2)}) collective-permute-start(bf16[96,768]{1,0:T(8,128)(2,1)S(1)} %get-tuple-element.102), channel_id=1, source_target_pairs={{0,8},{4,12},{8,16},{12,20},{16,24},{20,28},{24,0},{28,4},{1,9},{5... | collective-permute-start | bytes 442376 | tf_op jit(solution)/shard_map/ppermute | solution.py:100
  487.6 42.2 %all-reduce = (f32[768]{0:T(1024)}, f32[32,12]{0,1:T(8,128)}, f32[768]{0:T(1024)}, f32[768,4]{0,1:T(4,128)}) all-reduce(f32[768]{0:T(1024)S(1)} %get-tuple-element.74, f32[32,12]{0,1:T(8,128)S(1)} %dynamic_update_slice.3, f32[768]{0:T(1024)S(1)} %copy-done.33, ...), channel_id=1, replica_groups=mesh['dp'=8,'tensor'=4] {'dp','tensor'}, use_global_device_ids=true, to_apply=%region_17.18 | all-reduce | flops 4992 | bytes 39936 | tf_op jit(solution)/shard_map/psum | solution.py:568
  (310 shorter events, 180.4 us)
Async XLA Ops:
  10.2 66.0 %reduce-scatter.4.cloned.1.call-start = ((), (), s32[]{:S(2)}) async-start(), calls=%async_computation.4 | async-start | bytes 1966080 | tf_op jit(solution)/shard_map/reduce_scatter | solution.py:516
  46.5 155.3 %all-gather.6.cloned.1.call-start = ((), (), s32[]{:S(2)}) async-start(), calls=%async_computation.5 | async-start | bytes 3932160 | tf_op jit(solution)/shard_map/all_gather | solution.py:531
  79.7 246.7 %reduce-scatter.6.cloned.1.call-start = ((), (), s32[]{:S(2)}) async-start(), calls=%async_computation.6 | async-start | bytes 3932160 | tf_op jit(solution)/shard_map/reduce_scatter | solution.py:542
  85.8 37.9 %collective-permute-start.9 = (bf16[96,1536]{1,0:T(8,128)(2,1)S(1)}, bf16[96,1536]{1,0:T(8,128)(2,1)}, u32[]{:S(2)}, u32[]{:S(2)}) collective-permute-start(bf16[96,1536]{1,0:T(8,128)(2,1)S(1)} %get-tuple-element.106.refs_0_), channel_id=1, source_target_pairs={{0,24},{4,28},{8,0},{12,4},{16,8},{20,12},{24,16},{28,20},{1,25},{... | collective-permute-start | bytes 884744 | tf_op jit(solution)/shard_map/ppermute | solution.py:68
  87.3 37.9 %collective-permute-start.10 = (bf16[96,1536]{1,0:T(8,128)(2,1)S(1)}, bf16[96,1536]{1,0:T(8,128)(2,1)S(1)}, u32[]{:S(2)}, u32[]{:S(2)}) collective-permute-start(bf16[96,1536]{1,0:T(8,128)(2,1)S(1)} %get-tuple-element.106.refs_0_), channel_id=1, source_target_pairs={{0,4},{4,0},{8,12},{12,8},{16,20},{20,16},{24,28},{28,24},{1,5},{5... | collective-permute-start | bytes 884744 | tf_op jit(solution)/shard_map/ppermute | solution.py:69
  88.7 41.5 %collective-permute-start.14 = (bf16[96,1536]{1,0:T(8,128)(2,1)S(1)}, bf16[96,1536]{1,0:T(8,128)(2,1)S(1)}, u32[]{:S(2)}, u32[]{:S(2)}) collective-permute-start(bf16[96,1536]{1,0:T(8,128)(2,1)S(1)} %get-tuple-element.107.refs_1_), channel_id=1, source_target_pairs={{0,8},{4,12},{8,16},{12,20},{16,24},{20,28},{24,0},{28,4},{1,9},{5... | collective-permute-start | bytes 884744 | tf_op jit(solution)/shard_map/ppermute | solution.py:68
  93.9 49.3 %collective-permute-start.15 = (bf16[96,1536]{1,0:T(8,128)(2,1)S(1)}, bf16[96,1536]{1,0:T(8,128)(2,1)S(1)}, u32[]{:S(2)}, u32[]{:S(2)}) collective-permute-start(bf16[96,1536]{1,0:T(8,128)(2,1)S(1)} %get-tuple-element.107.refs_1_), channel_id=1, source_target_pairs={{0,16},{4,20},{8,24},{12,28},{16,0},{20,4},{24,8},{28,12},{1,17},{... | collective-permute-start | bytes 884744 | tf_op jit(solution)/shard_map/ppermute | solution.py:68
  130.3 38.3 %collective-permute-start.22 = (bf16[96,1536]{1,0:T(8,128)(2,1)S(1)}, bf16[96,1536]{1,0:T(8,128)(2,1)S(1)}, u32[]{:S(2)}, u32[]{:S(2)}) collective-permute-start(bf16[96,1536]{1,0:T(8,128)(2,1)S(1)} %get-tuple-element.108.refs_1_), channel_id=1, source_target_pairs={{0,16},{4,20},{8,24},{12,28},{16,0},{20,4},{24,8},{28,12},{1,17},{... | collective-permute-start | bytes 884744 | tf_op jit(solution)/shard_map/ppermute | solution.py:68
  200.3 41.7 %collective-permute-start.27 = (bf16[96,1536]{1,0:T(8,128)(2,1)}, bf16[96,1536]{1,0:T(8,128)(2,1)}, u32[]{:S(2)}, u32[]{:S(2)}) collective-permute-start(bf16[96,1536]{1,0:T(8,128)(2,1)} %copy-done.55), channel_id=1, source_target_pairs={{0,4},{4,0},{8,12},{12,8},{16,20},{20,16},{24,28},{28,24},{1,5},{5... | collective-permute-start | bytes 884744 | tf_op jit(solution)/shard_map/ppermute | solution.py:69
  212.3 45.3 %collective-permute-start.31 = (bf16[96,1536]{1,0:T(8,128)(2,1)}, bf16[96,1536]{1,0:T(8,128)(2,1)S(1)}, u32[]{:S(2)}, u32[]{:S(2)}) collective-permute-start(bf16[96,1536]{1,0:T(8,128)(2,1)} %get-tuple-element.105.refs_1_), channel_id=1, source_target_pairs={{0,4},{4,0},{8,12},{12,8},{16,20},{20,16},{24,28},{28,24},{1,5},{5... | collective-permute-start | bytes 884744 | tf_op jit(solution)/shard_map/ppermute | solution.py:69
  212.9 44.7 %collective-permute-start.32 = (bf16[96,1536]{1,0:T(8,128)(2,1)S(1)}, bf16[96,1536]{1,0:T(8,128)(2,1)S(1)}, u32[]{:S(2)}, u32[]{:S(2)}) collective-permute-start(bf16[96,1536]{1,0:T(8,128)(2,1)S(1)} %copy-done.50), channel_id=1, source_target_pairs={{0,4},{4,0},{8,12},{12,8},{16,20},{20,16},{24,28},{28,24},{1,5},{5... | collective-permute-start | bytes 884744 | tf_op jit(solution)/shard_map/ppermute | solution.py:69
  219.3 38.4 %collective-permute-start.33 = (bf16[96,1536]{1,0:T(8,128)(2,1)S(1)}, bf16[96,1536]{1,0:T(8,128)(2,1)S(1)}, u32[]{:S(2)}, u32[]{:S(2)}) collective-permute-start(bf16[96,1536]{1,0:T(8,128)(2,1)S(1)} %copy-done.54), channel_id=1, source_target_pairs={{0,4},{4,0},{8,12},{12,8},{16,20},{20,16},{24,28},{28,24},{1,5},{5... | collective-permute-start | bytes 884744 | tf_op jit(solution)/shard_map/ppermute | solution.py:69
  269.8 162.4 %all-gather.8.cloned.1.call-start = ((), (), s32[]{:S(2)}) async-start(), calls=%async_computation.7 | async-start | bytes 1966080 | tf_op jit(solution)/shard_map/all_gather | solution.py:550
  270.9 53.4 %collective-permute-start.43 = (bf16[4,96,1536]{2,1,0:T(8,128)(2,1)}, bf16[4,96,1536]{2,1,0:T(8,128)(2,1)S(1)}, u32[]{:S(2)}, u32[]{:S(2)}) collective-permute-start(bf16[4,96,1536]{2,1,0:T(8,128)(2,1)} %get-tuple-element.55), channel_id=1, source_target_pairs={{0,4},{4,0},{8,12},{12,8},{16,20},{20,16},{24,28},{28,24},{1,5},{5... | collective-permute-start | bytes 3538952 | tf_op jit(solution)/shard_map/ppermute | solution.py:95
  271.9 77.8 %collective-permute-start.47 = (bf16[4,96,1536]{2,1,0:T(8,128)(2,1)}, bf16[4,96,1536]{2,1,0:T(8,128)(2,1)}, u32[]{:S(2)}, u32[]{:S(2)}) collective-permute-start(bf16[4,96,1536]{2,1,0:T(8,128)(2,1)} %get-tuple-element.57), channel_id=1, source_target_pairs={{0,4},{4,0},{8,12},{12,8},{16,20},{20,16},{24,28},{28,24},{1,5},{5... | collective-permute-start | bytes 3538952 | tf_op jit(solution)/shard_map/ppermute | solution.py:95
  272.9 96.9 %collective-permute-start.51 = (bf16[4,96,1536]{2,1,0:T(8,128)(2,1)}, bf16[4,96,1536]{2,1,0:T(8,128)(2,1)}, u32[]{:S(2)}, u32[]{:S(2)}) collective-permute-start(bf16[4,96,1536]{2,1,0:T(8,128)(2,1)} %get-tuple-element.59), channel_id=1, source_target_pairs={{0,4},{4,0},{8,12},{12,8},{16,20},{20,16},{24,28},{28,24},{1,5},{5... | collective-permute-start | bytes 3538952 | tf_op jit(solution)/shard_map/ppermute | solution.py:95
  301.7 78.5 %collective-permute-start.40 = (bf16[96,1536]{1,0:T(8,128)(2,1)}, bf16[96,1536]{1,0:T(8,128)(2,1)}, u32[]{:S(2)}, u32[]{:S(2)}) collective-permute-start(bf16[96,1536]{1,0:T(8,128)(2,1)} %get-tuple-element.88), channel_id=1, source_target_pairs={{0,8},{4,12},{8,16},{12,20},{16,24},{20,28},{24,0},{28,4},{1,9},{5... | collective-permute-start | bytes 884744 | tf_op jit(solution)/shard_map/ppermute | solution.py:100
  307.4 76.2 %collective-permute-start.41 = (bf16[96,1536]{1,0:T(8,128)(2,1)}, bf16[96,1536]{1,0:T(8,128)(2,1)}, u32[]{:S(2)}, u32[]{:S(2)}) collective-permute-start(bf16[96,1536]{1,0:T(8,128)(2,1)} %get-tuple-element.90), channel_id=1, source_target_pairs={{0,16},{4,20},{8,24},{12,28},{16,0},{20,4},{24,8},{28,12},{1,17},{... | collective-permute-start | bytes 884744 | tf_op jit(solution)/shard_map/ppermute | solution.py:100
  324.3 59.4 %collective-permute-start.42 = (bf16[96,1536]{1,0:T(8,128)(2,1)}, bf16[96,1536]{1,0:T(8,128)(2,1)}, u32[]{:S(2)}, u32[]{:S(2)}) collective-permute-start(bf16[96,1536]{1,0:T(8,128)(2,1)} %get-tuple-element.89), channel_id=1, source_target_pairs={{0,24},{4,28},{8,0},{12,4},{16,8},{20,12},{24,16},{28,20},{1,25},{... | collective-permute-start | bytes 884744 | tf_op jit(solution)/shard_map/ppermute | solution.py:100
  331.9 154.3 %reduce-scatter.8.cloned.1.call-start = ((), (), s32[]{:S(2)}) async-start(), calls=%async_computation.8 | async-start | bytes 1966080 | tf_op jit(solution)/shard_map/reduce_scatter | solution.py:556
  383.6 46.4 %collective-permute-start.49 = (bf16[96,1536]{1,0:T(8,128)(2,1)S(1)}, bf16[96,1536]{1,0:T(8,128)(2,1)S(1)}, u32[]{:S(2)}, u32[]{:S(2)}) collective-permute-start(bf16[96,1536]{1,0:T(8,128)(2,1)S(1)} %get-tuple-element.96), channel_id=1, source_target_pairs={{0,16},{4,20},{8,24},{12,28},{16,0},{20,4},{24,8},{28,12},{1,17},{... | collective-permute-start | bytes 884744 | tf_op jit(solution)/shard_map/ppermute | solution.py:100
  385.8 44.3 %collective-permute-start.50 = (bf16[96,1536]{1,0:T(8,128)(2,1)S(1)}, bf16[96,1536]{1,0:T(8,128)(2,1)S(1)}, u32[]{:S(2)}, u32[]{:S(2)}) collective-permute-start(bf16[96,1536]{1,0:T(8,128)(2,1)S(1)} %get-tuple-element.95), channel_id=1, source_target_pairs={{0,24},{4,28},{8,0},{12,4},{16,8},{20,12},{24,16},{28,20},{1,25},{... | collective-permute-start | bytes 884744 | tf_op jit(solution)/shard_map/ppermute | solution.py:100
  393.9 54.4 %collective-permute-start.52 = (bf16[96,1536]{1,0:T(8,128)(2,1)}, bf16[96,1536]{1,0:T(8,128)(2,1)}, u32[]{:S(2)}, u32[]{:S(2)}) collective-permute-start(bf16[96,1536]{1,0:T(8,128)(2,1)} %get-tuple-element.97), channel_id=1, source_target_pairs={{0,8},{4,12},{8,16},{12,20},{16,24},{20,28},{24,0},{28,4},{1,9},{5... | collective-permute-start | bytes 884744 | tf_op jit(solution)/shard_map/ppermute | solution.py:100
  398.7 49.6 %collective-permute-start.53 = (bf16[96,1536]{1,0:T(8,128)(2,1)}, bf16[96,1536]{1,0:T(8,128)(2,1)}, u32[]{:S(2)}, u32[]{:S(2)}) collective-permute-start(bf16[96,1536]{1,0:T(8,128)(2,1)} %get-tuple-element.99), channel_id=1, source_target_pairs={{0,16},{4,20},{8,24},{12,28},{16,0},{20,4},{24,8},{28,12},{1,17},{... | collective-permute-start | bytes 884744 | tf_op jit(solution)/shard_map/ppermute | solution.py:100
  (106 other events, 2964.1 us)
Sparse Core Ops, SparseCore 0:
  10.4 22.3 all-gather.3
  46.7 29.5 reduce-scatter.3
  79.8 28.5 all-gather.5
  269.9 40.8 reduce-scatter.5
  332.1 23.0 all-gather.7
  447.3 32.3 reduce-scatter.7

commit v2 on v1

--- a/solution.py
+++ b/solution.py
@@ -157,7 +157,7 @@
             bias_ref[h, side] = tiles[h]
 
 
-def biased_scores(raw, gap, h, bias_ref, table_ref, first_key, key_start, query_block):
+def biased_scores(raw, gap, h, bias_ref, table_ref, first_key, key_start):
     far = table_ref[h, NBKT - 1]
     keys = key_start + iota((QT, QT), 0)
     if gap >= 2:
@@ -191,6 +191,40 @@
     return copies
 
 
+def attend_blocks(heads, seq, first_ref, table_ref, q_t, v_t, kn, bias_ref, s_ref, ctx_t, lse_ref, blocks):
+    for i in blocks:
+        cols = slice(i * QT, (i + 1) * QT)
+        first_key = first_ref[0:1, cols]
+        for h in range(heads):
+            band = slice(h * HD, (h + 1) * HD)
+            q_blk = q_t[band, cols]
+            peak = None
+            for j in range(i + 1):
+                raw = nn(kn[h, j * QT : (j + 1) * QT], q_blk)
+                s = biased_scores(raw, i - j, h, bias_ref, table_ref, first_key, j * QT)
+                s_ref[h, j] = s
+                top = jnp.max(s, axis=0, keepdims=True)
+                peak = top if peak is None else jnp.maximum(peak, top)
+            total = jnp.zeros((1, QT), F32)
+            acc = jnp.zeros((HD, QT), F32)
+            for j in range(i + 1):
+                p = jnp.exp(s_ref[h, j] - peak)
+                total = total + jnp.sum(p, axis=0, keepdims=True)
+                acc = acc + nn(v_t[band, j * QT : (j + 1) * QT], p.astype(BF))
+            ctx_t[band, cols] = (acc / total).astype(BF)
+            lse_ref[h : h + 1, cols] = peak + jnp.log(total)
+
+
+def project(heads, x, w_ref, qkv_ref, q_t, v_t, kn):
+    width = heads * HD
+    qkv = nn(x, w_ref[:, : 3 * width]).astype(BF)
+    qkv_ref[...] = qkv
+    q_t[...] = jnp.transpose(qkv[:, :width]) * jnp.asarray(1.0 / math.sqrt(HD), BF)
+    v_t[...] = jnp.transpose(qkv[:, 2 * width :])
+    for h in range(heads):
+        kn[h] = qkv[:, width + h * HD : width + (h + 1) * HD]
+
+
 def attend_kernel(heads, pieces, offsets_ref, table_ref, x_ref, first_ref, *refs):
     piece_refs = refs[:pieces]
     qkv_ref, ctx_ref, lse_ref, branch_ref, w_out_ref = refs[pieces : pieces + 5]
@@ -202,33 +236,11 @@
     for copy in copies:
         copy.wait()
     w_out_ref[...] = w_ref[...]
-    qkv = nn(x_ref[...], w_ref[:, : 3 * width]).astype(BF)
-    qkv_ref[...] = qkv
-    q_t[...] = jnp.transpose(qkv[:, :width]) * jnp.asarray(1.0 / math.sqrt(HD), BF)
-    v_t[...] = jnp.transpose(qkv[:, 2 * width :])
-    for h in range(heads):
-        kn[h] = qkv[:, width + h * HD : width + (h + 1) * HD]
-    for i in range(seq // QT):
-        cols = slice(i * QT, (i + 1) * QT)
-        first_key = first_ref[:, cols]
-        for h in range(heads):
-            band = slice(h * HD, (h + 1) * HD)
-            q_blk = q_t[band, cols]
-            peak = None
-            for j in range(i + 1):
-                raw = nn(kn[h, j * QT : (j + 1) * QT], q_blk)
-                s = biased_scores(raw, i - j, h, bias_ref, table_ref, first_key, j * QT, i)
-                s_ref[h, j] = s
-                top = jnp.max(s, axis=0, keepdims=True)
-                peak = top if peak is None else jnp.maximum(peak, top)
-            total = jnp.zeros((1, QT), F32)
-            acc = jnp.zeros((HD, QT), F32)
-            for j in range(i + 1):
-                p = jnp.exp(s_ref[h, j] - peak)
-                total = total + jnp.sum(p, axis=0, keepdims=True)
-                acc = acc + nn(v_t[band, j * QT : (j + 1) * QT], p.astype(BF))
-            ctx_t[band, cols] = (acc / total).astype(BF)
-            lse_ref[h : h + 1, cols] = peak + jnp.log(total)
+    project(heads, x_ref[...], w_ref, qkv_ref, q_t, v_t, kn)
+    blocks = range(seq // QT)
+    attend_blocks(
+        heads, seq, first_ref, table_ref, q_t, v_t, kn, bias_ref, s_ref, ctx_t, lse_ref, blocks
+    )
     ctx = jnp.transpose(ctx_t[...])
     ctx_ref[...] = ctx
     branch_ref[...] = nt(ctx, w_ref[:, 3 * width :]).astype(BF)
@@ -305,7 +317,7 @@
             for i in range(j, seq // QT):
                 cols = slice(i * QT, (i + 1) * QT)
                 raw = nn(kn[h, keys], q_t[band, cols])
-                s = biased_scores(raw, i - j, h, bias_ref, table_ref, first_ref[:, cols], j * QT, i)
+                s = biased_scores(raw, i - j, h, bias_ref, table_ref, first_ref[0:1, cols], j * QT)
                 p = jnp.exp(s - lse_ref[h : h + 1, cols])
                 dp = nn(vn[h, keys], dc_t[band, cols])
                 ds = p * (dp - delta_ref[h : h + 1, cols])
@@ -396,7 +408,16 @@
     w_ref, acc_ref, sem = refs[pieces + 1 + len(blocks) :]
     hidden = w_ref.shape[1] // 2
     length = xd_ref.shape[0]
-    copies = load_rows(piece_refs, offsets_ref, w_ref, sem)
+    if len(piece_refs[0].shape) == 3:
+        whole = piece_refs[0]
+        copies = [
+            pltpu.make_async_copy(whole.at[2 * e], w_ref.at[:, :hidden], sem.at[0]),
+            pltpu.make_async_copy(whole.at[2 * e + 1], w_ref.at[:, hidden:], sem.at[1]),
+        ]
+        for copy in copies:
+            copy.start()
+    else:
+        copies = load_rows(piece_refs, offsets_ref, w_ref, sem)
     if has_terms:
         terms_ref[...] = terms_in[...]
     else:
@@ -434,7 +455,7 @@
 def expert(e, plan, offsets, goffs, xd, slot_row, slot_col, terms, pieces, size):
     length, both = xd.shape
     model = both // 2
-    hidden2 = pieces[0].shape[1]
+    hidden2 = 2 * pieces[0].shape[2] if pieces[0].ndim == 3 else pieces[0].shape[1]
     n = len(pieces)
     vmem = pl.BlockSpec(memory_space=pltpu.VMEM)
     smem = pl.BlockSpec(memory_space=pltpu.SMEM)
@@ -452,13 +473,319 @@
         scratch_shapes=[
             pltpu.VMEM((model, hidden2), BF),
             pltpu.VMEM((model, hidden2), F32),
-            pltpu.SemaphoreType.DMA((n,)),
+            pltpu.SemaphoreType.DMA((max(n, 2),)),
         ],
         compiler_params=pltpu.CompilerParams(vmem_limit_bytes=VMEM_MAX),
         cost_estimate=pl.CostEstimate(flops=3 * 10**9, bytes_accessed=10**7, transcendentals=10**6),
         name=f"expert_{e}",
     )(plan, offsets, goffs, xd, slot_row, slot_col, *extra, *pieces)
     return out[0], out[1:]
+
+
+MESH = pl.DeviceIdType.MESH
+PIECES = 1 + 2 * E
+T_SEMS = 32
+W_SEMS = 7 * PIECES
+
+
+class Here:
+    def __init__(self):
+        self.d = lax.axis_index("dp")
+        self.t = lax.axis_index("tensor")
+        self.z, self.y = self.d // 2, self.d % 2
+        self.x, self.c = self.t // 2, self.t % 2
+        self.core = {"dp": self.d, "tensor": 2 * self.x + 1 - self.c}
+        self.side = {"dp": self.d, "tensor": 2 * (1 - self.x) + self.c}
+        self.over = {"dp": 2 * self.z + 1 - self.y, "tensor": self.t}
+
+    def z_dp(self, k):
+        return 2 * ((self.z + 4 + k) % 4) + self.y
+
+    def z_peer(self, k):
+        return {"dp": self.z_dp(k), "tensor": self.t}
+
+    def greet(self):
+        barrier = pltpu.get_barrier_semaphore()
+        peers = [self.core, self.side, self.over] + [self.z_peer(k) for k in (1, 2, 3)]
+        for peer in peers:
+            pl.semaphore_signal(barrier, inc=1, device_id=peer, device_id_type=MESH)
+        pl.semaphore_wait(barrier, len(peers))
+
+
+class Wire:
+    def __init__(self, send, recv):
+        self.send, self.recv, self.sent = send, recv, []
+
+    def __call__(self, src, dst, peer):
+        k = len(self.sent)
+        copy = pltpu.make_async_remote_copy(
+            src_ref=src, dst_ref=dst, send_sem=self.send.at[k], recv_sem=self.recv.at[k],
+            device_id=peer, device_id_type=MESH,
+        )
+        copy.start()
+        self.sent.append(copy)
+        return copy
+
+    def close(self):
+        for copy in self.sent:
+            copy.wait_send()
+
+
+class Rows:
+    def __init__(self, here, wire, buf, rows, part, parts):
+        self.here, self.wire, self.buf = here, wire, buf
+        self.rows, self.size = rows, rows // parts
+        self.shift = part * self.size
+
+    def at(self, t):
+        return self.buf.at[pl.ds(pl.multiple_of(t * self.rows + self.shift, 16), self.size)]
+
+    def start(self):
+        mine = self.at(self.here.t)
+        self.far = self.wire(mine, mine, self.here.side)
+        self.near = self.wire(mine, mine, self.here.core)
+
+    def forward(self):
+        self.far.wait_recv()
+        theirs = self.at(2 * (1 - self.here.x) + self.here.c)
+        self.last = self.wire(theirs, theirs, self.here.core)
+
+    def finish(self):
+        self.near.wait_recv()
+        self.last.wait_recv()
+
+
+class Sums:
+    def __init__(self, here, wire, src, landed, out, back, rows, part, parts):
+        self.here, self.wire, self.src = here, wire, src
+        self.landed, self.out, self.back = landed, out, back
+        self.rows, self.size = rows, rows // parts
+        self.shift = part * self.size
+        self.part = part
+
+    def at(self, t):
+        return pl.ds(pl.multiple_of(t * self.rows + self.shift, 16), self.size)
+
+    def start(self):
+        h = self.here
+        self.copies = []
+        for slot, x in ((0, 1 - h.x), (1, h.x)):
+            src = self.src.at[self.at(2 * x + 1 - h.c)]
+            self.copies.append(self.wire(src, self.landed.at[slot, self.part], h.core))
+
+    def cross(self):
+        h = self.here
+        self.copies[0].wait_recv()
+        mine = self.src[self.at(2 * (1 - h.x) + h.c)].astype(F32)
+        self.out[self.part] = (mine + self.landed[0, self.part].astype(F32)).astype(BF)
+        self.last = self.wire(self.out.at[self.part], self.back.at[self.part], h.side)
+
+    def total(self):
+        h = self.here
+        self.copies[1].wait_recv()
+        near = self.src[self.at(2 * h.x + h.c)].astype(F32) + self.landed[1, self.part].astype(F32)
+        self.last.wait_recv()
+        return near + self.back[self.part].astype(F32)
+
+
+class Weights:
+    def __init__(self, here, wire, own_sem, sources, target):
+        self.here, self.wire, self.own_sem = here, wire, own_sem
+        self.sources, self.target = sources, target
+        self.z, self.over, self.own = {}, {}, {}
+
+    def at(self, p, dp):
+        rows = self.sources[p].shape[0]
+        return self.target(p, pl.ds(pl.multiple_of(dp * rows, 16), rows))
+
+    def start(self, p):
+        if p >= PIECES:
+            return
+        h, src = self.here, self.sources[p]
+        dst = self.at(p, h.d)
+        self.z[p] = [self.wire(src, dst, h.z_peer(k)) for k in (1, 2, 3)]
+        self.over[p] = [self.wire(src, dst, h.over)]
+        self.own[p] = pltpu.make_async_copy(src, dst, self.own_sem.at[p])
+        self.own[p].start()
+
+    def forward(self, p):
+        if p >= PIECES:
+            return
+        h = self.here
+        for k, copy in zip((1, 2, 3), self.z[p]):
+            copy.wait_recv()
+            part = self.at(p, h.z_dp(-k))
+            self.over[p].append(self.wire(part, part, h.over))
+
+    def finish(self, p):
+        for copy in self.over[p]:
+            copy.wait_recv()
+        self.own[p].wait()
+
+
+def normed(values, gain):
+    inverse = lax.rsqrt(jnp.mean(values * values, axis=-1, keepdims=True) + EPSILON)
+    return values * inverse * gain
+
+
+def front_kernel(
+    heads, table_ref, tokens_ref, cot_ref, seg_ref, route_ref, gain_a_ref, gain_f_ref, router_ref,
+    wq_ref, wk_ref, wv_ref, wo_ref, w_in_ref, w_out_ref,
+    attn_rows, qkv_ref, ctx_ref, lse_ref, w_attn, first_ref, attended_ref, x_rows, d_rows, experts,
+    attn_shard, outer_shard, tab_ref, q_t, v_t, kn, bias_ref, s_ref, ctx_t, cot_rows, branch,
+    landed, out, back, t_send, t_recv, w_send, w_recv, own_sem,
+):
+    h = Here()
+    width = heads * HD
+    seq = attn_rows.shape[0]
+    rows = tokens_ref.shape[0]
+    wire = Wire(t_send, t_recv)
+    sources = [attn_shard]
+    for e in range(E):
+        sources += [w_in_ref.at[e], outer_shard.at[e]]
+
+    def target(p, at):
+        return w_attn.at[at] if p == 0 else experts.at[p - 1, at]
+
+    weights = Weights(h, Wire(w_send, w_recv), own_sem, sources, target)
+    attn_shard[:, :width] = wq_ref[...]
+    attn_shard[:, width : 2 * width] = wk_ref[...]
+    attn_shard[:, 2 * width : 3 * width] = wv_ref[...]
+    attn_shard[:, 3 * width :] = jnp.transpose(wo_ref[...])
+    h.greet()
+    weights.start(0)
+
+    half = rows // 2
+    gathers = [Rows(h, wire, attn_rows, rows, part, 2) for part in range(2)]
+    gain_a = gain_a_ref[...].astype(F32)
+    for part in range(2):
+        at = pl.ds(pl.multiple_of(h.t * rows + part * half, 16), half)
+        attn_rows[at] = normed(tokens_ref[part * half : (part + 1) * half], gain_a).astype(BF)
+        gathers[part].start()
+    own = pl.ds(pl.multiple_of(h.t * rows, 16), rows)
+    cot_rows[own] = cot_ref[...].astype(BF)
+    for hd in range(heads):
+        for b in range(NBKT):
+            tab_ref[hd, b] = table_ref[b, h.t * heads + hd]
+    fill_bias(bias_ref, tab_ref, heads)
+    segments = seg_ref[...]
+    first = jnp.zeros(segments.shape, jnp.int32)
+    for s in range(1, 5):
+        first = jnp.where(segments >= s, jnp.sum(jnp.where(segments < s, 1, 0)), first)
+    first_ref[...] = jnp.broadcast_to(first, first_ref.shape)
+    for e in range(E):
+        outer_shard[e] = jnp.transpose(w_out_ref[e])
+    gathers[0].forward()
+    gathers[1].forward()
+    weights.forward(0)
+    weights.start(1)
+    weights.start(2)
+    gathers[0].finish()
+    gathers[1].finish()
+    cots = Rows(h, wire, cot_rows, rows, 0, 1)
+    cots.start()
+    weights.finish(0)
+
+    project(heads, attn_rows[...], w_attn, qkv_ref, q_t, v_t, kn)
+    state = (first_ref, tab_ref, q_t, v_t, kn, bias_ref, s_ref, ctx_t, lse_ref)
+    attend_blocks(heads, seq, *state, range(0, 3))
+    cots.forward()
+    weights.forward(1)
+    weights.start(3)
+    attend_blocks(heads, seq, *state, range(3, seq // QT))
+    ctx = jnp.transpose(ctx_t[...])
+    ctx_ref[...] = ctx
+    branch[...] = nt(ctx, w_attn[:, 3 * width :]).astype(BF)
+    sums = [Sums(h, wire, branch, landed, out, back, rows, part, 2) for part in range(2)]
+    for part in range(2):
+        sums[part].start()
+    for part in range(2):
+        sums[part].cross()
+    weights.forward(2)
+    weights.start(4)
+    gathers = [Rows(h, wire, x_rows, rows, part, 2) for part in range(2)]
+    gain_f = gain_f_ref[...].astype(F32)
+    for part in range(2):
+        at = slice(part * half, (part + 1) * half)
+        attended = tokens_ref[at] + sums[part].total()
+        attended_ref[at] = attended
+        x_rows[pl.ds(pl.multiple_of(h.t * rows + part * half, 16), half)] = normed(
+            attended, gain_f
+        ).astype(BF)
+        gathers[part].start()
+    weights.forward(3)
+    weights.start(5)
+    for part in range(2):
+        gathers[part].forward()
+    cots.finish()
+    for part in range(2):
+        gathers[part].finish()
+    logits = nn(x_rows[...], router_ref[...])
+    raised = jnp.exp(logits - jnp.max(logits, axis=1, keepdims=True))
+    chosen = jnp.where(route_ref[...] == iota(logits.shape, 1), raised, 0.0)
+    gate = jnp.sum(chosen, axis=1, keepdims=True) / jnp.sum(raised, axis=1, keepdims=True)
+    d_rows[...] = (cot_rows[...].astype(F32) * gate).astype(BF)
+    for p in range(4, PIECES):
+        weights.forward(p)
+        weights.start(p + 2)
+    for p in range(1, PIECES):
+        weights.finish(p)
+    wire.close()
+    weights.wire.close()
+
+
+def front(table, tokens, cot, segments, routes, gain_a, gain_f, router, wq, wk, wv, wo, w_in, w_out):
+    rows, model = tokens.shape
+    seq = segments.shape[1]
+    width = wq.shape[1]
+    heads = width // HD
+    vmem = pl.BlockSpec(memory_space=pltpu.VMEM)
+    smem = pl.BlockSpec(memory_space=pltpu.SMEM)
+    hbm = pl.BlockSpec(memory_space=pl.ANY)
+    shard = wq.shape[0]
+    return pl.pallas_call(
+        functools.partial(front_kernel, heads),
+        out_shape=(
+            jax.ShapeDtypeStruct((seq, model), BF),
+            jax.ShapeDtypeStruct((seq, 3 * width), BF),
+            jax.ShapeDtypeStruct((seq, width), BF),
+            jax.ShapeDtypeStruct((8, seq), F32),
+            jax.ShapeDtypeStruct((model, 4 * width), BF),
+            jax.ShapeDtypeStruct((8, seq), jnp.int32),
+            jax.ShapeDtypeStruct((rows, model), F32),
+            jax.ShapeDtypeStruct((seq, model), BF),
+            jax.ShapeDtypeStruct((seq, model), BF),
+            jax.ShapeDtypeStruct((2 * E, model, w_in.shape[2]), BF),
+        ),
+        in_specs=[smem] + [vmem] * 11 + [hbm, vmem],
+        out_specs=(vmem,) * 9 + (hbm,),
+        scratch_shapes=[
+            pltpu.VMEM((shard, model), BF),
+            pltpu.VMEM((E, shard, w_in.shape[2]), BF),
+            pltpu.SMEM((heads, NBKT), F32),
+            pltpu.VMEM((width, seq), BF),
+            pltpu.VMEM((width, seq), BF),
+            pltpu.VMEM((heads, seq, HD), BF),
+            pltpu.VMEM((heads, 2, HALF, HALF), F32),
+            pltpu.VMEM((heads, seq // QT, QT, QT), F32),
+            pltpu.VMEM((width, seq), BF),
+            pltpu.VMEM((seq, model), BF),
+            pltpu.VMEM((seq, model), BF),
+            pltpu.VMEM((2, 2, rows // 2, model), BF),
+            pltpu.VMEM((2, rows // 2, model), BF),
+            pltpu.VMEM((2, rows // 2, model), BF),
+            pltpu.SemaphoreType.DMA((T_SEMS,)),
+            pltpu.SemaphoreType.DMA((T_SEMS,)),
+            pltpu.SemaphoreType.DMA((W_SEMS,)),
+            pltpu.SemaphoreType.DMA((W_SEMS,)),
+            pltpu.SemaphoreType.DMA((PIECES,)),
+        ],
+        compiler_params=pltpu.CompilerParams(
+            vmem_limit_bytes=VMEM_MAX, collective_id=1, has_side_effects=True
+        ),
+        cost_estimate=pl.CostEstimate(flops=4 * 10**9, bytes_accessed=10**8, transcendentals=2 * 10**6),
+        name="front",
+    )(table, tokens, cot, segments, routes, gain_a, gain_f, router, wq, wk, wv, wo, w_in, w_out)
 
 
 def rms_apply(values, gain_vec):
@@ -493,29 +820,39 @@
     hidden = w_inner.shape[2]
     shard_rows = w_query.shape[0]
 
-    attn_shard = jnp.concatenate([w_query, w_key, w_value, jnp.transpose(w_output)], axis=1)
-    attn_pieces, offsets = gather_dp(attn_shard, size)
-    both_shard = jnp.concatenate([w_inner, jnp.transpose(w_outer, (0, 2, 1))], axis=2)
-    expert_pieces = [gather_dp(both_shard[e], size)[0] for e in range(E)]
     goffs = send_offsets(shard_rows, size)
-
     route_row = jnp.reshape(routes, (1, seq_len))
     slot_row, slot_col, plan = make_plan(route_row)
-    counts = [jnp.sum((segments < s).astype(jnp.int32)) for s in range(1, 5)]
-    first_key = jnp.zeros_like(segments)
-    for s in range(1, 5):
-        first_key = jnp.where(segments >= s, counts[s - 1], first_key)
-    first_key = first_key[None, :]
     table = jnp.transpose(
         lax.dynamic_slice_in_dim(rel_table.astype(F32), part_index * heads, heads, 1)
     )
-
-    normed_attn, norm_one_pull = jax.vjp(rms_apply, tokens, gain_attn.astype(F32))
-    attn_rows = lax.all_gather(normed_attn.astype(BF), "tensor", axis=0, tiled=True)
-    qkv, ctx, lse, branch, w_attn = attend(attn_rows, attn_pieces, offsets, table, first_key, heads)
-    attended = tokens + lax.psum_scatter(
-        branch, "tensor", scatter_dimension=0, tiled=True
-    ).astype(F32)
+    if size == 8:
+        attn_rows, qkv, ctx, lse, w_attn, first_key, attended, x_rows, d_rows, experts = front(
+            rel_table.astype(F32), tokens, cotangent, segments[None, :], routes, gain_attn[None, :],
+            gain_ffn[None, :], w_router, w_query, w_key, w_value, w_output, w_inner, w_outer,
+        )
+        expert_pieces = [[experts]] * E
+        offsets = jnp.zeros((1,), jnp.int32)
+        normed_attn, norm_one_pull = jax.vjp(rms_apply, tokens, gain_attn.astype(F32))
+        xd = jnp.concatenate([x_rows, d_rows], axis=1)
+    else:
+        attn_shard = jnp.concatenate([w_query, w_key, w_value, jnp.transpose(w_output)], axis=1)
+        attn_pieces, offsets = gather_dp(attn_shard, size)
+        both_shard = jnp.concatenate([w_inner, jnp.transpose(w_outer, (0, 2, 1))], axis=2)
+        expert_pieces = [gather_dp(both_shard[e], size)[0] for e in range(E)]
+        counts = [jnp.sum((segments < s).astype(jnp.int32)) for s in range(1, 5)]
+        first_key = jnp.zeros_like(segments)
+        for s in range(1, 5):
+            first_key = jnp.where(segments >= s, counts[s - 1], first_key)
+        first_key = first_key[None, :]
+        normed_attn, norm_one_pull = jax.vjp(rms_apply, tokens, gain_attn.astype(F32))
+        attn_rows = lax.all_gather(normed_attn.astype(BF), "tensor", axis=0, tiled=True)
+        qkv, ctx, lse, branch, w_attn = attend(
+            attn_rows, attn_pieces, offsets, table, first_key, heads
+        )
+        attended = tokens + lax.psum_scatter(
+            branch, "tensor", scatter_dimension=0, tiled=True
+        ).astype(F32)
 
     normed_ffn, norm_two_pull = jax.vjp(rms_apply, attended, gain_ffn.astype(F32))
     ffn_in = normed_ffn.astype(BF)
@@ -527,10 +864,11 @@
         return jnp.sum(jax.nn.softmax(logits, axis=-1) * route_mask, axis=-1)
 
     gate_weight, gate_pull = jax.vjp(gate_of, ffn_in.astype(F32), w_router.astype(F32))
-    d_expert = (cotangent * gate_weight[:, None]).astype(BF)
-    xd = lax.all_gather(
-        jnp.concatenate([ffn_in, d_expert], axis=1), "tensor", axis=0, tiled=True
-    )
+    if size != 8:
+        d_expert = (cotangent * gate_weight[:, None]).astype(BF)
+        xd = lax.all_gather(
+            jnp.concatenate([ffn_in, d_expert], axis=1), "tensor", axis=0, tiled=True
+        )
 
     terms = None
     expert_sums = []

time: 545 us -> 480 us (0.88)
  waiting for transfers between devices: 193 us -> 70.9 us
  Pallas kernels: 80.1 us -> 200 us
  starting transfers between devices: 157 us -> 99.5 us
  other arithmetic: 37.7 us -> 26.7 us
    pallas_call x1, Pallas kernels: 11 us -> 135 us  [front(): pl.pallas_call(functools.partial(front_kernel, heads), out_shape=(jax.Sha...]
    ppermute x35 -> x0, starting transfers between devices: 88.9 us -> none  [the longest x15 63.5 us: gather_dp(): own = [shard] + [lax.ppermute(shard, 'dp', z_shift(k)) for k in (1, 2, 3)]]
    ppermute x35 -> x0, waiting for transfers between devices: 59.4 us -> none  [the longest x15 36 us: gather_dp(): own = [shard] + [lax.ppermute(shard, 'dp', z_shift(k)) for k in (1, 2, 3)]]
    ppermute x5, waiting for transfers between devices: 78.7 us -> 39.2 us  [reduce_dp(): got = lax.ppermute(other, 'dp', Y_SWAP)]
    ppermute x15, starting transfers between devices: 62.1 us -> 94.8 us  [reduce_dp(): arrived.append(lax.ppermute(pair, 'dp', z_shift(k)))]
    reduce_scatter x1 -> x0, waiting for transfers between devices: 28.4 us -> none  [per_device(): lax.psum_scatter(branch, 'tensor', scatter_dimension=0, tiled=True)]
  transfers between devices with their start and end apart: 61 -> 23, of which waited for: 23 -> 11; matrix products, arithmetic and copies ran while one was open for 6% -> 6% of each run, Pallas kernels for 11% -> 3%
where the time goes in v2:
time: 480 us; the launch traced here: 471 us
  Pallas kernels  200 us (42%)
  starting transfers between devices  99.5 us (21%)
  waiting for transfers between devices  70.9 us (15%)
  blocking collectives  42.9 us (9%)
  other arithmetic  26.7 us (6%)
  between operations  14.6 us (3%)
  local copies, waits for them, and re-layouts  13.7 us (3%)
    pallas_call x1, Pallas kernels, front(): pl.pallas_call(functools.partial(front_kernel, heads), out_shape=(jax.Sha...  135 us
    ppermute x15, starting transfers between devices, reduce_dp(): arrived.append(lax.ppermute(pair, 'dp', z_shift(k)))  94.8 us
    pallas_call x4, Pallas kernels, expert(): pl.pallas_call(functools.partial(expert_kernel, e, n, blocks), out_shape=...  48.2 us
    psum x1, blocking collectives, per_device(): lax.psum((grad_gain_one, grad_gain_two, grad_router_local, grad_table_ful...  42.9 us
    ppermute x5, waiting for transfers between devices, reduce_dp(): got = lax.ppermute(other, 'dp', Y_SWAP)  39.2 us
    ppermute x15, waiting for transfers between devices, reduce_dp(): arrived.append(lax.ppermute(pair, 'dp', z_shift(k)))  28.5 us
    pallas_call x1, Pallas kernels, attend_back(): pl.pallas_call(functools.partial(attend_back_kernel, heads, blocks), out_...  15 us
  transfers between devices with their start and end apart: 23, of which 11 were waited for; matrix products, arithmetic and copies ran while one was open for 6% of the time, Pallas kernels for 3%

profile of v2, /device:TPU:0, one launch (start us, length us, event | category | flops | bytes accessed | tf_op | source)
XLA Modules:
  0.0 470.7 jit_solution(6611297185464297612)
XLA Ops:
  14.0 135.1 %front.1 = (bf16[1024,768]{1,0:T(8,128)(2,1)}, bf16[1024,576]{1,0:T(8,128)(2,1)}, bf16[1024,192]{1,0:T(8,128)(2,1)}, f32[8,1024]{1,0:T(8,128)}, bf16[768,768]{1,...) custom-call(f32[32,12]{1,0:T(8,128)} %copy.27.table_ref, ...), custom_call_target="tpu_custom_call" | custom-call | flops 4000000000 | bytes 100000000 | tf_op jit(solution)/shard_map/front/pallas_call | solution.py:746
  154.5 10.3 %expert_0.1 = (bf16[1024,1536]{1,0:T(8,128)(2,1)}, bf16[4,96,1536]{2,1,0:T(8,128)(2,1)}, bf16[4,96,1536]{2,1,0:T(8,128)(2,1)}) custom-call(s32[8]{0:T(128)} %get-tuple-element.42.plan_ref, s32[1]{0:T(128)} %constant.87.clone.1.offsets_ref, s32[8]{0:T(128)} %broadcast_multiply_fusion.goffs_ref.offs_ref, bf16[1024,1536]{1,0:T(8,128)(2,1)} %copy-done, ...), custom_call_target="tpu_custom_call" | custom-call | flops 3000000000 | bytes 10000000 | tf_op jit(solution)/shard_map/expert_0/pallas_call | solution.py:465
  164.9 11.3 %expert_1.1 = (bf16[1024,1536]{1,0:T(8,128)(2,1)}, bf16[4,96,1536]{2,1,0:T(8,128)(2,1)}, bf16[4,96,1536]{2,1,0:T(8,128)(2,1)}) custom-call(s32[8]{0:T(128)} %get-tuple-element.42.plan_ref, s32[1]{0:T(128)} %constant.87.clone.1.offsets_ref, s32[8]{0:T(128)} %broadcast_multiply_fusion.goffs_ref.offs_ref, bf16[1024,1536]{1,0:T(8,128)(2,1)} %copy-done, ...), custom_call_target="tpu_custom_call" | custom-call | flops 3000000000 | bytes 10000000 | tf_op jit(solution)/shard_map/expert_1/pallas_call | solution.py:465
  176.1 15.3 %expert_2.1 = (bf16[1024,1536]{1,0:T(8,128)(2,1)}, bf16[4,96,1536]{2,1,0:T(8,128)(2,1)}, bf16[4,96,1536]{2,1,0:T(8,128)(2,1)}) custom-call(s32[8]{0:T(128)} %get-tuple-element.42.plan_ref, s32[1]{0:T(128)} %constant.87.clone.1.offsets_ref, s32[8]{0:T(128)} %broadcast_multiply_fusion.goffs_ref.offs_ref, bf16[1024,1536]{1,0:T(8,128)(2,1)} %copy-done, ...), custom_call_target="tpu_custom_call" | custom-call | flops 3000000000 | bytes 10000000 | tf_op jit(solution)/shard_map/expert_2/pallas_call | solution.py:465
  191.5 11.3 %expert_3.1 = (bf16[1024,1536]{1,0:T(8,128)(2,1)}, bf16[4,96,1536]{2,1,0:T(8,128)(2,1)}, bf16[4,96,1536]{2,1,0:T(8,128)(2,1)}) custom-call(s32[8]{0:T(128)} %get-tuple-element.42.plan_ref, s32[1]{0:T(128)} %constant.87.clone.1.offsets_ref, s32[8]{0:T(128)} %broadcast_multiply_fusion.goffs_ref.offs_ref, bf16[1024,1536]{1,0:T(8,128)(2,1)} %copy-done, ...), custom_call_target="tpu_custom_call" | custom-call | flops 3000000000 | bytes 10000000 | tf_op jit(solution)/shard_map/expert_3/pallas_call | solution.py:465
  209.6 22.5 %collective-permute-done.4 = bf16[4,96,1536]{2,1,0:T(8,128)(2,1)} collective-permute-done((bf16[4,96,1536]{2,1,0:T(8,128)(2,1)}, bf16[4,96,1536]{2,1,0:T(8,128)(2,1)}, u32[]{:S(2)}, u32[]{:S(2)}) %collective-permute-start.4) | collective-permute-done | bytes 1179680 | tf_op jit(solution)/shard_map/ppermute | solution.py:95
  234.6 3.6 collective-permute-start.5
  238.2 15.4 %collective-permute-start.6 = (bf16[96,1536]{1,0:T(8,128)(2,1)}, bf16[96,1536]{1,0:T(8,128)(2,1)}, u32[]{:S(2)}, u32[]{:S(2)}) collective-permute-start(bf16[96,1536]{1,0:T(8,128)(2,1)} %get-tuple-element.96), channel_id=1, source_target_pairs={{0,16},{4,20},{8,24},{12,28},{16,0},{20,4},{24,8},{28,12},{1,17},{... | collective-permute-start | bytes 884744 | tf_op jit(solution)/shard_map/ppermute | solution.py:100
  253.6 3.7 collective-permute-done.8
  257.4 18.5 %collective-permute-start.7 = (bf16[96,1536]{1,0:T(8,128)(2,1)}, bf16[96,1536]{1,0:T(8,128)(2,1)}, u32[]{:S(2)}, u32[]{:S(2)}) collective-permute-start(bf16[96,1536]{1,0:T(8,128)(2,1)} %get-tuple-element.95), channel_id=1, source_target_pairs={{0,24},{4,28},{8,0},{12,4},{16,8},{20,12},{24,16},{28,20},{1,25},{... | collective-permute-start | bytes 884744 | tf_op jit(solution)/shard_map/ppermute | solution.py:100
  283.1 14.6 %collective-permute-start.10 = (bf16[96,1536]{1,0:T(8,128)(2,1)}, bf16[96,1536]{1,0:T(8,128)(2,1)S(1)}, u32[]{:S(2)}, u32[]{:S(2)}) collective-permute-start(bf16[96,1536]{1,0:T(8,128)(2,1)} %get-tuple-element.99), channel_id=1, source_target_pairs={{0,16},{4,20},{8,24},{12,28},{16,0},{20,4},{24,8},{28,12},{1,17},{... | collective-permute-start | bytes 884744 | tf_op jit(solution)/shard_map/ppermute | solution.py:100
  299.5 5.3 %collective-permute-done.16 = bf16[4,96,1536]{2,1,0:T(8,128)(2,1)} collective-permute-done((bf16[4,96,1536]{2,1,0:T(8,128)(2,1)}, bf16[4,96,1536]{2,1,0:T(8,128)(2,1)}, u32[]{:S(2)}, u32[]{:S(2)}) %collective-permute-start.16) | collective-permute-done | bytes 1179680 | tf_op jit(solution)/shard_map/ppermute | solution.py:95
  304.8 17.8 %collective-permute-start.11 = (bf16[96,1536]{1,0:T(8,128)(2,1)S(1)}, bf16[96,1536]{1,0:T(8,128)(2,1)S(1)}, u32[]{:S(2)}, u32[]{:S(2)}) collective-permute-start(bf16[96,1536]{1,0:T(8,128)(2,1)S(1)} %copy-done.11), channel_id=1, source_target_pairs={{0,24},{4,28},{8,0},{12,4},{16,8},{20,12},{24,16},{28,20},{1,25},{... | collective-permute-start | bytes 884744 | tf_op jit(solution)/shard_map/ppermute | solution.py:100
  324.9 4.3 collective-permute-start.14
  332.8 4.0 collective-permute-done.9
  338.0 5.0 %collective-permute-done.13 = bf16[96,1536]{1,0:T(8,128)(2,1)S(1)} collective-permute-done((bf16[96,1536]{1,0:T(8,128)(2,1)S(1)}, bf16[96,1536]{1,0:T(8,128)(2,1)S(1)}, u32[]{:S(2)}, u32[]{:S(2)}) %collective-permute-start.13) | collective-permute-done | bytes 294944 | tf_op jit(solution)/shard_map/ppermute | solution.py:100
  343.0 5.7 %collective-permute-start.19 = (bf16[96,1536]{1,0:T(8,128)(2,1)S(1)}, bf16[96,1536]{1,0:T(8,128)(2,1)}, u32[]{:S(2)}, u32[]{:S(2)}) collective-permute-start(bf16[96,1536]{1,0:T(8,128)(2,1)S(1)} %get-tuple-element.104), channel_id=1, source_target_pairs={{0,24},{4,28},{8,0},{12,4},{16,8},{20,12},{24,16},{28,20},{1,25},{... | collective-permute-start | bytes 884744 | tf_op jit(solution)/shard_map/ppermute | solution.py:100
  348.7 13.8 %collective-permute-done.14 = bf16[96,1536]{1,0:T(8,128)(2,1)S(1)} collective-permute-done((bf16[96,1536]{1,0:T(8,128)(2,1)S(1)}, bf16[96,1536]{1,0:T(8,128)(2,1)S(1)}, u32[]{:S(2)}, u32[]{:S(2)}) %collective-permute-start.14) | collective-permute-done | bytes 294944 | tf_op jit(solution)/shard_map/ppermute | solution.py:100
  364.5 15.0 %attend_back.1 = (bf16[1024,768]{1,0:T(8,128)(2,1)}, f32[8,128]{1,0:T(8,128)}, bf16[4,96,768]{2,1,0:T(8,128)(2,1)}, bf16[4,96,768]{2,1,0:T(8,128)(2,1)}) custom-call(s32[8]{0:T(128)} %broadcast_multiply_fusion.goffs_ref.offs_ref, f32[3,32]{1,0:T(4,128)} %dynamic-slice_bitcast_fusion.table_ref, bf16[1024,768]{1,0:T(8,128)(2,1)} %all-gather.2.cloned.1.call-done.d_ref, ...), custom_call_target="tpu_custom_call" | custom-call | flops 10000000000 | bytes 10000000 | tf_op jit(solution)/shard_map/attend_back/pallas_call | solution.py:369
  385.7 7.6 %collective-permute-done = bf16[4,96,768]{2,1,0:T(8,128)(2,1)S(1)} collective-permute-done((bf16[4,96,768]{2,1,0:T(8,128)(2,1)S(1)}, bf16[4,96,768]{2,1,0:T(8,128)(2,1)S(1)}, u32[]{:S(2)}, u32[]{:S(2)}) %collective-permute-start) | collective-permute-done | bytes 589856 | tf_op jit(solution)/shard_map/ppermute | solution.py:95
  394.1 10.4 %collective-permute-start.1 = (bf16[96,768]{1,0:T(8,128)(2,1)}, bf16[96,768]{1,0:T(8,128)(2,1)S(1)}, u32[]{:S(2)}, u32[]{:S(2)}) collective-permute-start(bf16[96,768]{1,0:T(8,128)(2,1)} %get-tuple-element.106), channel_id=1, source_target_pairs={{0,8},{4,12},{8,16},{12,20},{16,24},{20,28},{24,0},{28,4},{1,9},{5... | collective-permute-start | bytes 442376 | tf_op jit(solution)/shard_map/ppermute | solution.py:100
  408.9 3.3 collective-permute-done.2
  415.4 3.1 reduce-scatter.5.cloned.1.call-done
  419.9 42.9 %all-reduce = (f32[768]{0:T(1024)}, f32[32,12]{0,1:T(8,128)}, f32[768]{0:T(1024)}, f32[768,4]{0,1:T(4,128)}) all-reduce(f32[768]{0:T(1024)S(1)} %get-tuple-element.84, f32[32,12]{0,1:T(8,128)S(1)} %dynamic_update_slice.3, f32[768]{0:T(1024)S(1)} %copy-done.17, ...), channel_id=1, replica_groups=mesh['dp'=8,'tensor'=4] {'dp','tensor'}, use_global_device_ids=true, to_apply=%region_12.13 | all-reduce | flops 4992 | bytes 39936 | tf_op jit(solution)/shard_map/psum | solution.py:906
  (157 shorter events, 56.3 us)
Async XLA Ops:
  7.2 270.8 %reduce-scatter.3.cloned.1.call-start = ((), (), s32[]{:S(2)}) async-start(), calls=%async_computation.2 | async-start | bytes 3932160 | tf_op jit(solution)/shard_map/reduce_scatter | solution.py:880
  202.8 161.7 %all-gather.2.cloned.1.call-start = ((), (), s32[]{:S(2)}) async-start(), calls=%async_computation.3 | async-start | bytes 1966080 | tf_op jit(solution)/shard_map/all_gather | solution.py:888
  202.8 29.3 %collective-permute-start.4 = (bf16[4,96,1536]{2,1,0:T(8,128)(2,1)}, bf16[4,96,1536]{2,1,0:T(8,128)(2,1)}, u32[]{:S(2)}, u32[]{:S(2)}) collective-permute-start(bf16[4,96,1536]{2,1,0:T(8,128)(2,1)} %get-tuple-element.63), channel_id=1, source_target_pairs={{0,4},{4,0},{8,12},{12,8},{16,20},{20,16},{24,28},{28,24},{1,5},{5... | collective-permute-start | bytes 3538952 | tf_op jit(solution)/shard_map/ppermute | solution.py:95
  203.4 54.0 %collective-permute-start.8 = (bf16[4,96,1536]{2,1,0:T(8,128)(2,1)}, bf16[4,96,1536]{2,1,0:T(8,128)(2,1)}, u32[]{:S(2)}, u32[]{:S(2)}) collective-permute-start(bf16[4,96,1536]{2,1,0:T(8,128)(2,1)} %get-tuple-element.65), channel_id=1, source_target_pairs={{0,4},{4,0},{8,12},{12,8},{16,20},{20,16},{24,28},{28,24},{1,5},{5... | collective-permute-start | bytes 3538952 | tf_op jit(solution)/shard_map/ppermute | solution.py:95
  204.9 78.2 %collective-permute-start.12 = (bf16[4,96,1536]{2,1,0:T(8,128)(2,1)}, bf16[4,96,1536]{2,1,0:T(8,128)(2,1)}, u32[]{:S(2)}, u32[]{:S(2)}) collective-permute-start(bf16[4,96,1536]{2,1,0:T(8,128)(2,1)} %get-tuple-element.67), channel_id=1, source_target_pairs={{0,4},{4,0},{8,12},{12,8},{16,20},{20,16},{24,28},{28,24},{1,5},{5... | collective-permute-start | bytes 3538952 | tf_op jit(solution)/shard_map/ppermute | solution.py:95
  205.4 99.3 %collective-permute-start.16 = (bf16[4,96,1536]{2,1,0:T(8,128)(2,1)}, bf16[4,96,1536]{2,1,0:T(8,128)(2,1)}, u32[]{:S(2)}, u32[]{:S(2)}) collective-permute-start(bf16[4,96,1536]{2,1,0:T(8,128)(2,1)} %get-tuple-element.69), channel_id=1, source_target_pairs={{0,4},{4,0},{8,12},{12,8},{16,20},{20,16},{24,28},{28,24},{1,5},{5... | collective-permute-start | bytes 3538952 | tf_op jit(solution)/shard_map/ppermute | solution.py:95
  207.1 72.5 %copy-start.21 = (f32[256]{0:T(256)}, f32[256]{0:T(256)S(1)}, u32[]{:S(2)}) copy-start(f32[256]{0:T(256)S(1)} %fusion.38) | copy-start | bytes 3076
  234.6 90.2 %collective-permute-start.5 = (bf16[96,1536]{1,0:T(8,128)(2,1)}, bf16[96,1536]{1,0:T(8,128)(2,1)}, u32[]{:S(2)}, u32[]{:S(2)}) collective-permute-start(bf16[96,1536]{1,0:T(8,128)(2,1)} %get-tuple-element.94), channel_id=1, source_target_pairs={{0,8},{4,12},{8,16},{12,20},{16,24},{20,28},{24,0},{28,4},{1,9},{5... | collective-permute-start | bytes 884744 | tf_op jit(solution)/shard_map/ppermute | solution.py:100
  238.2 86.6 %collective-permute-start.6 = (bf16[96,1536]{1,0:T(8,128)(2,1)}, bf16[96,1536]{1,0:T(8,128)(2,1)}, u32[]{:S(2)}, u32[]{:S(2)}) collective-permute-start(bf16[96,1536]{1,0:T(8,128)(2,1)} %get-tuple-element.96), channel_id=1, source_target_pairs={{0,16},{4,20},{8,24},{12,28},{16,0},{20,4},{24,8},{28,12},{1,17},{... | collective-permute-start | bytes 884744 | tf_op jit(solution)/shard_map/ppermute | solution.py:100
  257.4 67.5 %collective-permute-start.7 = (bf16[96,1536]{1,0:T(8,128)(2,1)}, bf16[96,1536]{1,0:T(8,128)(2,1)}, u32[]{:S(2)}, u32[]{:S(2)}) collective-permute-start(bf16[96,1536]{1,0:T(8,128)(2,1)} %get-tuple-element.95), channel_id=1, source_target_pairs={{0,24},{4,28},{8,0},{12,4},{16,8},{20,12},{24,16},{28,20},{1,25},{... | collective-permute-start | bytes 884744 | tf_op jit(solution)/shard_map/ppermute | solution.py:100
  283.0 135.5 %reduce-scatter.5.cloned.1.call-start = ((), (), s32[]{:S(2)}) async-start(), calls=%async_computation.4 | async-start | bytes 1966080 | tf_op jit(solution)/shard_map/reduce_scatter | solution.py:894
  283.1 47.6 %collective-permute-start.10 = (bf16[96,1536]{1,0:T(8,128)(2,1)}, bf16[96,1536]{1,0:T(8,128)(2,1)S(1)}, u32[]{:S(2)}, u32[]{:S(2)}) collective-permute-start(bf16[96,1536]{1,0:T(8,128)(2,1)} %get-tuple-element.99), channel_id=1, source_target_pairs={{0,16},{4,20},{8,24},{12,28},{16,0},{20,4},{24,8},{28,12},{1,17},{... | collective-permute-start | bytes 884744 | tf_op jit(solution)/shard_map/ppermute | solution.py:100
  304.8 26.0 %collective-permute-start.11 = (bf16[96,1536]{1,0:T(8,128)(2,1)S(1)}, bf16[96,1536]{1,0:T(8,128)(2,1)S(1)}, u32[]{:S(2)}, u32[]{:S(2)}) collective-permute-start(bf16[96,1536]{1,0:T(8,128)(2,1)S(1)} %copy-done.11), channel_id=1, source_target_pairs={{0,24},{4,28},{8,0},{12,4},{16,8},{20,12},{24,16},{28,20},{1,25},{... | collective-permute-start | bytes 884744 | tf_op jit(solution)/shard_map/ppermute | solution.py:100
  324.8 12.0 %collective-permute-start.9 = (bf16[96,1536]{1,0:T(8,128)(2,1)S(1)}, bf16[96,1536]{1,0:T(8,128)(2,1)S(1)}, u32[]{:S(2)}, u32[]{:S(2)}) collective-permute-start(bf16[96,1536]{1,0:T(8,128)(2,1)S(1)} %copy-done.10), channel_id=1, source_target_pairs={{0,8},{4,12},{8,16},{12,20},{16,24},{20,28},{24,0},{28,4},{1,9},{5... | collective-permute-start | bytes 884744 | tf_op jit(solution)/shard_map/ppermute | solution.py:100
  324.8 18.2 %collective-permute-start.13 = (bf16[96,1536]{1,0:T(8,128)(2,1)S(1)}, bf16[96,1536]{1,0:T(8,128)(2,1)S(1)}, u32[]{:S(2)}, u32[]{:S(2)}) collective-permute-start(bf16[96,1536]{1,0:T(8,128)(2,1)S(1)} %get-tuple-element.100), channel_id=1, source_target_pairs={{0,8},{4,12},{8,16},{12,20},{16,24},{20,28},{24,0},{28,4},{1,9},{5... | collective-permute-start | bytes 884744 | tf_op jit(solution)/shard_map/ppermute | solution.py:100
  324.9 37.5 %collective-permute-start.14 = (bf16[96,1536]{1,0:T(8,128)(2,1)S(1)}, bf16[96,1536]{1,0:T(8,128)(2,1)S(1)}, u32[]{:S(2)}, u32[]{:S(2)}) collective-permute-start(bf16[96,1536]{1,0:T(8,128)(2,1)S(1)} %get-tuple-element.102), channel_id=1, source_target_pairs={{0,16},{4,20},{8,24},{12,28},{16,0},{20,4},{24,8},{28,12},{1,17},{... | collective-permute-start | bytes 884744 | tf_op jit(solution)/shard_map/ppermute | solution.py:100
  330.7 31.7 %collective-permute-start.15 = (bf16[96,1536]{1,0:T(8,128)(2,1)S(1)}, bf16[96,1536]{1,0:T(8,128)(2,1)S(1)}, u32[]{:S(2)}, u32[]{:S(2)}) collective-permute-start(bf16[96,1536]{1,0:T(8,128)(2,1)S(1)} %get-tuple-element.101), channel_id=1, source_target_pairs={{0,24},{4,28},{8,0},{12,4},{16,8},{20,12},{24,16},{28,20},{1,25},{... | collective-permute-start | bytes 884744 | tf_op jit(solution)/shard_map/ppermute | solution.py:100
  330.8 49.9 %collective-permute-start.17 = (bf16[96,1536]{1,0:T(8,128)(2,1)}, bf16[96,1536]{1,0:T(8,128)(2,1)}, u32[]{:S(2)}, u32[]{:S(2)}) collective-permute-start(bf16[96,1536]{1,0:T(8,128)(2,1)} %get-tuple-element.103), channel_id=1, source_target_pairs={{0,8},{4,12},{8,16},{12,20},{16,24},{20,28},{24,0},{28,4},{1,9},{5... | collective-permute-start | bytes 884744 | tf_op jit(solution)/shard_map/ppermute | solution.py:100
  336.8 43.9 %collective-permute-start.18 = (bf16[96,1536]{1,0:T(8,128)(2,1)}, bf16[96,1536]{1,0:T(8,128)(2,1)}, u32[]{:S(2)}, u32[]{:S(2)}) collective-permute-start(bf16[96,1536]{1,0:T(8,128)(2,1)} %get-tuple-element.105), channel_id=1, source_target_pairs={{0,16},{4,20},{8,24},{12,28},{16,0},{20,4},{24,8},{28,12},{1,17},{... | collective-permute-start | bytes 884744 | tf_op jit(solution)/shard_map/ppermute | solution.py:100
  343.0 37.7 %collective-permute-start.19 = (bf16[96,1536]{1,0:T(8,128)(2,1)S(1)}, bf16[96,1536]{1,0:T(8,128)(2,1)}, u32[]{:S(2)}, u32[]{:S(2)}) collective-permute-start(bf16[96,1536]{1,0:T(8,128)(2,1)S(1)} %get-tuple-element.104), channel_id=1, source_target_pairs={{0,24},{4,28},{8,0},{12,4},{16,8},{20,12},{24,16},{28,20},{1,25},{... | collective-permute-start | bytes 884744 | tf_op jit(solution)/shard_map/ppermute | solution.py:100
  383.4 9.9 %collective-permute-start = (bf16[4,96,768]{2,1,0:T(8,128)(2,1)S(1)}, bf16[4,96,768]{2,1,0:T(8,128)(2,1)S(1)}, u32[]{:S(2)}, u32[]{:S(2)}) collective-permute-start(bf16[4,96,768]{2,1,0:T(8,128)(2,1)S(1)} %copy-done.32), channel_id=1, source_target_pairs={{0,4},{4,0},{8,12},{12,8},{16,20},{20,16},{24,28},{28,24},{1,5},{5... | collective-permute-start | bytes 1769480 | tf_op jit(solution)/shard_map/ppermute | solution.py:95
  394.1 14.8 %collective-permute-start.1 = (bf16[96,768]{1,0:T(8,128)(2,1)}, bf16[96,768]{1,0:T(8,128)(2,1)S(1)}, u32[]{:S(2)}, u32[]{:S(2)}) collective-permute-start(bf16[96,768]{1,0:T(8,128)(2,1)} %get-tuple-element.106), channel_id=1, source_target_pairs={{0,8},{4,12},{8,16},{12,20},{16,24},{20,28},{24,0},{28,4},{1,9},{5... | collective-permute-start | bytes 442376 | tf_op jit(solution)/shard_map/ppermute | solution.py:100
  404.5 7.6 %collective-permute-start.2 = (bf16[96,768]{1,0:T(8,128)(2,1)S(1)}, bf16[96,768]{1,0:T(8,128)(2,1)S(1)}, u32[]{:S(2)}, u32[]{:S(2)}) collective-permute-start(bf16[96,768]{1,0:T(8,128)(2,1)S(1)} %get-tuple-element.108), channel_id=1, source_target_pairs={{0,16},{4,20},{8,24},{12,28},{16,0},{20,4},{24,8},{28,12},{1,17},{... | collective-permute-start | bytes 442376 | tf_op jit(solution)/shard_map/ppermute | solution.py:100
  406.1 6.8 %collective-permute-start.3 = (bf16[96,768]{1,0:T(8,128)(2,1)S(1)}, bf16[96,768]{1,0:T(8,128)(2,1)}, u32[]{:S(2)}, u32[]{:S(2)}) collective-permute-start(bf16[96,768]{1,0:T(8,128)(2,1)S(1)} %get-tuple-element.107), channel_id=1, source_target_pairs={{0,24},{4,28},{8,0},{12,4},{16,8},{20,12},{24,16},{28,20},{1,25},{... | collective-permute-start | bytes 442376 | tf_op jit(solution)/shard_map/ppermute | solution.py:100
  (32 other events, 385.3 us)
Sparse Core Ops, SparseCore 0:
  202.9 54.3 reduce-scatter.2
  283.2 18.1 all-gather.1
  379.7 38.8 reduce-scatter.4
